TPU v7x, 256 devices: a whole 4x4x8 slice. The times are simulated.
256 devices in a mesh: section: 4 (over x), feat: 32 (over z, y), row: 2 (over core).
Axes of the slice: x: 4, y: 4, z: 8, core: 2. Of those that a mesh axis runs over, the one named last changes fastest.
Arguments:
- target_ids: int32 [8], replicated, may hold values from 0 to 16383
- target_pos: int32 [8], replicated, may hold values from 0 to 31
- target_gain: float32 [4608], replicated, may hold values from 0.1 to 1.9
- target_scale: float32 [32], replicated, may hold values from 0.3 to 3
- encoder: bfloat16 [16384, 4608], P(('feat', 'row')), may hold values from -6 to 6
- post_gain: float32 [4, 4608], P('section'), may hold values from 0.1 to 1.9
- post_scale: float32 [4, 32], P('section'), may hold values from 0.3 to 3
- out_proj: bfloat16 [4, 32, 128, 4608], P('section', 'feat'), may hold values from -0.09375 to 0.09375
- pattern: bfloat16 [4, 32, 32, 32], P('section', 'feat'), may hold values from 0 to 1, as said below
- value_proj: bfloat16 [4, 32, 4608, 128], P('section', 'feat'), may hold values from -0.1875 to 0.1875
- pre_gain: float32 [4, 4608], P('section'), may hold values from 0.1 to 1.9
- pre_scale: float32 [4, 32], P('section'), may hold values from 0.3 to 3
- decoder: bfloat16 [4, 2, 8192, 4608], P('section', None, 'feat'), may hold values from -0.09375 to 0.09375
- block_ids: int32 [4, 512, 128], P('section', 'feat'), may hold values from 0 to 255
- block_pos: int32 [4, 512], P('section', 'feat'), may hold values from 0 to 31
- block_act: float32 [4, 512, 128], P('section', 'feat'), may hold values from 0 to 4, as said below
- block_count: int32 [4, 32], P('section', 'feat'), may hold values from 1 to 16, as said below
Outputs:
- attributions: float32 [4, 8, 512, 128], P('section', 'row', 'feat')
- gradients: bfloat16 [4, 8, 32, 4608], P('section', 'row', None, 'feat')
Inputs may be any that keep to these rules, and one draw needn't show every extreme that they name: Each head's pattern is zero above the diagonal and its rows sum to one up to rounding. `block_act`: rows of activation 0 in a live block are padding. Owner o's blocks of layer l are the slots o * 16 to o * 16 + block_count[l, o] - 1; later slots hold entries without meaning. In every layer some owner has exactly 16 live blocks.
All inputs are finite; a program needn't handle non-finite values.
Results may differ from a plain program's by a relative error of at most 0.035.
Values may be sent and summed in bfloat16 or wider, within the bound.
A program may use at most 128 MiB of HBM per device.

v0:
```python
import jax
import jax.numpy as jnp
from jax import lax
from jax.sharding import PartitionSpec as P


def shifted(value, axis, steps):
    count = lax.axis_size(axis)
    initial, last = (max(0, -steps), min(count, count - steps))
    return lax.ppermute(value, axis, [(source, source + steps) for source in range(initial, last)])


def head_terms(
    full_in,
    post_gain_row,
    post_scale_row,
    out_weights,
    mix_weights,
    value_weights,
    pre_gain_row,
    pre_scale_row,
):
    scaled = (
        full_in.astype(jnp.float32) * post_gain_row[None, None, :] * post_scale_row[None, :, None]
    ).astype(jnp.bfloat16)
    head_in = jnp.einsum(
        "tsd,hed->tshe", scaled, out_weights, preferred_element_type=jnp.float32
    ).astype(jnp.bfloat16)
    head_mix = jnp.einsum(
        "hqp,tqhe->tphe", mix_weights, head_in, preferred_element_type=jnp.float32
    ).astype(jnp.bfloat16)
    summed = jnp.einsum(
        "tphe,hde->tpd", head_mix, value_weights, preferred_element_type=jnp.float32
    )
    return summed * pre_gain_row[None, None, :] * pre_scale_row[None, :, None]


def feature_scores(full_out, full_in, dec_layer, ids_layer, pos_layer, act_layer, live_count):
    target_rows = full_out.shape[0]
    positions = full_out.shape[1]
    block_slots = ids_layer.shape[0]
    block_width = ids_layer.shape[1]
    shard_rows = dec_layer.shape[1]
    scores_pos = jnp.einsum(
        "tpd,fd->tpf", full_out, dec_layer[0], preferred_element_type=jnp.float32
    )
    scores_pos = scores_pos + jnp.einsum(
        "tpd,fd->tpf", full_in, dec_layer[1], preferred_element_type=jnp.float32
    )
    flat_scores = scores_pos.reshape(target_rows, positions * shard_rows)
    flat_index = (pos_layer[:, None] * shard_rows + ids_layer).reshape(block_slots * block_width)
    picked = jnp.take(flat_scores, flat_index, axis=1).reshape(
        target_rows, block_slots, block_width
    )
    live_blocks = jnp.arange(block_slots) < live_count
    return jnp.where(live_blocks[None, :, None], picked * act_layer[None], jnp.zeros_like(picked))


def body(
    target_ids,
    target_pos,
    target_gain,
    target_scale,
    encoder,
    post_gain,
    post_scale,
    out_proj,
    pattern,
    value_proj,
    pre_gain,
    pre_scale,
    decoder,
    block_ids,
    block_pos,
    block_act,
    block_count,
):
    section_count = lax.axis_size("section")
    section_index = lax.axis_index("section")
    feat_count = lax.axis_size("feat")
    feat_index = lax.axis_index("feat")
    row_count = lax.axis_size("row")
    row_index = lax.axis_index("row")
    model_width = encoder.shape[1]
    part_width = model_width // feat_count
    target_count = target_ids.shape[0] // row_count
    positions = target_scale.shape[0]
    dict_rows = encoder.shape[0]
    block_slots = block_pos.shape[1]
    block_width = block_ids.shape[2]
    owner_index = target_ids // dict_rows
    local_ids = target_ids - owner_index * dict_rows
    picked_rows = jnp.take(encoder, local_ids, axis=0).astype(jnp.float32)
    fetched = jnp.where((owner_index == lax.axis_index(("feat", "row")))[:, None], picked_rows, 0.0)
    own_pos = lax.dynamic_slice_in_dim(target_pos, row_index * target_count, target_count, 0)
    hit_scale = (jnp.arange(positions)[None, :] == own_pos[:, None]).astype(
        jnp.float32
    ) * target_scale[None, :]
    arranged = fetched.reshape(row_count, target_count, feat_count, part_width)
    arranged = arranged.transpose(2, 0, 1, 3).reshape(
        feat_count * row_count * target_count, part_width
    )
    own_rows = lax.psum_scatter(arranged, ("feat", "row"), scatter_dimension=0, tiled=True)
    gain_part = lax.dynamic_slice_in_dim(target_gain, feat_index * part_width, part_width, 0)
    top_rows = (hit_scale[:, :, None] * (own_rows * gain_part[None, :])[:, None, :]).astype(
        jnp.bfloat16
    )
    group_count = 1
    per_group = target_count // group_count
    received = jnp.zeros((per_group, positions, top_rows.shape[2]), jnp.bfloat16)
    score_out = jnp.zeros((target_count, block_slots, block_width), jnp.float32)
    grad_out = jnp.zeros((target_count, positions, part_width), jnp.bfloat16)
    tick_count = group_count + section_count - 1
    for tick_num in range(tick_count):
        group_num = tick_num - (section_count - 1 - section_index)
        is_valid = (group_num >= 0) & (group_num < group_count)
        current = jnp.where(section_index == section_count - 1, top_rows, received)
        full_in = lax.all_gather(current, "feat", axis=2, tiled=True)
        head_term = head_terms(
            full_in,
            post_gain[0],
            post_scale[0],
            out_proj[0],
            pattern[0],
            value_proj[0],
            pre_gain[0],
            pre_scale[0],
        )
        head_sum = lax.psum_scatter(
            head_term.astype(jnp.bfloat16), "feat", scatter_dimension=2, tiled=True
        ).astype(jnp.float32)
        part_out = (current.astype(jnp.float32) + head_sum).astype(jnp.bfloat16)
        full_out = lax.all_gather(part_out, "feat", axis=2, tiled=True)
        scores_now = feature_scores(
            full_out,
            full_in,
            decoder[0],
            block_ids[0],
            block_pos[0],
            block_act[0],
            block_count[0, 0],
        )
        score_old = score_out
        score_out = jnp.where(is_valid, scores_now, score_old)
        grad_old = grad_out
        grad_out = jnp.where(is_valid, part_out, grad_old)
        if tick_num + 1 < tick_count:
            received = shifted(part_out, "section", -1)
    return (score_out[None], grad_out[None])


def solution(mesh):
    in_specs = (
        P(),
        P(),
        P(),
        P(),
        P(("feat", "row"), None),
        P("section", None),
        P("section", None),
        P("section", "feat", None, None),
        P("section", "feat", None, None),
        P("section", "feat", None, None),
        P("section", None),
        P("section", None),
        P("section", None, "feat", None),
        P("section", "feat", None),
        P("section", "feat"),
        P("section", "feat", None),
        P("section", "feat"),
    )
    out_specs = (P("section", "row", "feat", None), P("section", "row", None, "feat"))
    return jax.shard_map(body, mesh=mesh, in_specs=in_specs, out_specs=out_specs, check_vma=False)
```

profile of v0, /device:TPU:1, one launch (start us, length us, event | category | flops | bytes accessed | tf_op | source)
XLA Modules:
  0.0 1799.1 jit_solution(2861317664941628273)
XLA Ops:
  12.2 1.3 dynamic-slice
  14.9 175.7 %all-reduce.3.cloned.1.call-done = f32[256,144]{1,0:T(8,128)} async-done(((f32[256,144]{1,0:T(8,128)}), f32[256,144]{1,0:T(8,128)}) %all-reduce.3.cloned.1.call-update) | async-done | bytes 147472
  191.5 0.9 fusion.87
  192.6 79.0 %all-gather.9.cloned.1.call-done = bf16[4,32,4608]{1,0,2:T(4,128)(2,1)} async-done(((bf16[4,32,144]{1,0,2:T(4,128)(2,1)}), bf16[4,32,4608]{1,0,2:T(4,128)(2,1)}) %all-gather.9.cloned.1.call-update) | async-done | bytes 1179664 | tf_op jit(solution)/shard_map/all_gather | solution.py:118
  271.6 6.0 copy.78
  277.6 2.2 fusion.77
  280.5 4.9 copy.119
  285.5 6.4 reshape.323
  292.0 197.2 %reduce-scatter.13.cloned.1.call-done = bf16[144,128]{1,0:T(8,128)(2,1)} async-done(((bf16[4608,128]{1,0:T(8,128)(2,1)}), bf16[144,128]{1,0:T(8,128)(2,1)}) %reduce-scatter.13.cloned.1.call-update) | async-done | bytes 36880
  489.2 0.9 reshape.324
  490.3 1.3 collective-permute-start
  491.6 4.6 collective-permute-done
  497.1 85.8 %all-gather.11.cloned.1.call-done = bf16[4,32,4608]{1,0,2:T(4,128)(2,1)} async-done(((bf16[4,32,144]{1,0,2:T(4,128)(2,1)}), bf16[4,32,4608]{1,0,2:T(4,128)(2,1)}) %all-gather.11.cloned.1.call-update) | async-done | bytes 1179664 | tf_op jit(solution)/shard_map/all_gather | solution.py:118
  582.9 6.0 copy.81
  588.9 1.0 copy-done.9
  590.0 1.8 fusion.74
  592.4 5.0 copy.121
  597.4 6.4 reshape.325
  603.9 197.3 %reduce-scatter.15.cloned.1.call-done = bf16[144,128]{1,0:T(8,128)(2,1)} async-done(((bf16[4608,128]{1,0:T(8,128)(2,1)}), bf16[144,128]{1,0:T(8,128)(2,1)}) %reduce-scatter.15.cloned.1.call-update) | async-done | bytes 36880
  801.2 0.9 reshape.326
  802.3 1.3 collective-permute-start.1
  803.6 4.6 collective-permute-done.1
  809.2 85.8 %all-gather.13.cloned.1.call-done = bf16[4,32,4608]{1,0,2:T(4,128)(2,1)} async-done(((bf16[4,32,144]{1,0,2:T(4,128)(2,1)}), bf16[4,32,4608]{1,0,2:T(4,128)(2,1)}) %all-gather.13.cloned.1.call-update) | async-done | bytes 1179664 | tf_op jit(solution)/shard_map/all_gather | solution.py:118
  895.0 6.0 copy.84
  901.0 1.0 copy-done.11
  902.1 1.8 fusion.71
  904.5 5.0 copy.123
  909.5 6.4 reshape.327
  916.0 197.2 %reduce-scatter.17.cloned.1.call-done = bf16[144,128]{1,0:T(8,128)(2,1)} async-done(((bf16[4608,128]{1,0:T(8,128)(2,1)}), bf16[144,128]{1,0:T(8,128)(2,1)}) %reduce-scatter.17.cloned.1.call-update) | async-done | bytes 36880
  1114.3 1.3 collective-permute-start.2
  1115.6 4.6 collective-permute-done.2
  1120.2 0.9 fusion.84
  1121.4 85.6 %all-gather.15.cloned.1.call-done = bf16[4,32,4608]{1,0,2:T(4,128)(2,1)} async-done(((bf16[4,32,144]{1,0,2:T(4,128)(2,1)}), bf16[4,32,4608]{1,0,2:T(4,128)(2,1)}) %all-gather.15.cloned.1.call-update) | async-done | bytes 1179664 | tf_op jit(solution)/shard_map/all_gather | solution.py:118
  1207.0 6.0 copy.87
  1213.0 1.1 copy-done.13
  1214.0 1.8 fusion.68
  1216.5 5.0 copy.125
  1221.5 6.5 reshape.329
  1230.8 194.5 %reduce-scatter.19.cloned.1.call-done = bf16[144,128]{1,0:T(8,128)(2,1)} async-done(((bf16[4608,128]{1,0:T(8,128)(2,1)}), bf16[144,128]{1,0:T(8,128)(2,1)}) %reduce-scatter.19.cloned.1.call-update) | async-done | bytes 36880
  1426.2 1.0 select_bitcast_fusion.1
  1427.3 85.3 %all-gather.23.cloned.1.call-done = bf16[4,32,4608]{1,0,2:T(4,128)(2,1)} async-done(((bf16[4,32,144]{1,0,2:T(4,128)(2,1)}), bf16[4,32,4608]{1,0,2:T(4,128)(2,1)}) %all-gather.23.cloned.1.call-update) | async-done | bytes 1179664 | tf_op jit(solution)/shard_map/all_gather | solution.py:133
  1512.5 4.5 fusion.8
  1517.0 2.5 fusion.65
  1519.6 2.7 copy.118
  1522.3 9.7 gather_fusion.4
  1532.0 64.3 %all-gather.21.cloned.1.call-done = bf16[4,32,4608]{1,0,2:T(4,128)(2,1)} async-done(((bf16[4,32,144]{1,0,2:T(4,128)(2,1)}), bf16[4,32,4608]{1,0,2:T(4,128)(2,1)}) %all-gather.21.cloned.1.call-update) | async-done | bytes 1179664 | tf_op jit(solution)/shard_map/all_gather | solution.py:133
  1596.3 4.5 fusion.10
  1600.8 2.5 fusion.62
  1603.3 2.7 copy.117
  1606.0 9.7 gather_fusion.3
  1615.7 64.2 %all-gather.19.cloned.1.call-done = bf16[4,32,4608]{1,0,2:T(4,128)(2,1)} async-done(((bf16[4,32,144]{1,0,2:T(4,128)(2,1)}), bf16[4,32,4608]{1,0,2:T(4,128)(2,1)}) %all-gather.19.cloned.1.call-update) | async-done | bytes 1179664 | tf_op jit(solution)/shard_map/all_gather | solution.py:133
  1679.9 4.5 fusion.12
  1684.4 2.5 fusion.59
  1686.9 2.8 copy.116
  1689.7 9.8 gather_fusion.2
  1700.2 63.4 %all-gather.17.cloned.1.call-done = bf16[4,32,4608]{1,0,2:T(4,128)(2,1)} async-done(((bf16[4,32,144]{1,0,2:T(4,128)(2,1)}), bf16[4,32,4608]{1,0,2:T(4,128)(2,1)}) %all-gather.17.cloned.1.call-update) | async-done | bytes 1179664 | tf_op jit(solution)/shard_map/all_gather | solution.py:133
  1763.6 4.5 fusion.14
  1768.1 2.5 fusion.56
  1770.7 2.7 copy.115
  1773.4 9.7 gather_fusion.1
  1783.1 3.7 broadcast_select_fusion.3
  1786.8 1.6 copy.93
  1788.4 1.6 copy.97
  1789.9 1.6 copy.101
  (105 shorter events, 17.9 us)
Async XLA Ops:
  7.2 1.8 copy-start
  7.2 185.3 %copy-start.18 = (f32[1,4608]{1,0:T(1,128)S(1)}, f32[1,4608]{1,0:T(1,128)}, u32[]{:S(2)}) copy-start(f32[1,4608]{1,0:T(1,128)} %param.24) | copy-start | bytes 55300
  7.2 185.3 %copy-start.19 = (f32[1,4608]{1,0:T(1,128)S(1)}, f32[1,4608]{1,0:T(1,128)}, u32[]{:S(2)}) copy-start(f32[1,4608]{1,0:T(1,128)} %param.29) | copy-start | bytes 55300
  7.2 183.4 %all-reduce.3.cloned.1.call-start = ((), (), s32[]{:S(2)}) async-start(), calls=%async_computation.16 | async-start | bytes 524288
  10.7 260.9 %all-gather.9.cloned.1.call-start = ((), (), s32[]{:S(2)}) async-start(), calls=%async_computation.4 | async-start | bytes 4866048 | tf_op jit(solution)/shard_map/all_gather | solution.py:118
  192.4 296.8 %reduce-scatter.13.cloned.1.call-start = ((), (), s32[]{:S(2)}) async-start(), calls=%async_computation.12 | async-start | bytes 1216512
  192.6 85.0 %copy-start.22 = (f32[1,32]{1,0:T(1,128)S(1)}, f32[1,32]{1,0:T(1,128)}, u32[]{:S(2)}) copy-start(f32[1,32]{1,0:T(1,128)} %param.25) | copy-start | bytes 388
  277.6 2.3 copy-start.7
  277.6 2.3 copy-start.2
  277.6 2.3 copy-start.16
  277.6 2.3 copy-start.21
  292.0 291.0 %all-gather.11.cloned.1.call-start = ((), (), s32[]{:S(2)}) async-start(), calls=%async_computation.5 | async-start | bytes 4866048 | tf_op jit(solution)/shard_map/all_gather | solution.py:118
  490.3 98.6 %copy-start.15 = (bf16[4,32,144]{1,0,2:T(4,128)(2,1)}, bf16[4,32,144]{1,0,2:T(4,128)(2,1)S(1)}, u32[]{:S(2)}) copy-start(bf16[4,32,144]{1,0,2:T(4,128)(2,1)S(1)} %add_convert_fusion.3) | copy-start | bytes 110596
  490.3 5.9 collective-permute-start
  497.1 304.1 %reduce-scatter.15.cloned.1.call-start = ((), (), s32[]{:S(2)}) async-start(), calls=%async_computation.13 | async-start | bytes 1216512
  588.9 1.0 copy-start.9
  603.8 291.1 %all-gather.13.cloned.1.call-start = ((), (), s32[]{:S(2)}) async-start(), calls=%async_computation.6 | async-start | bytes 4866048 | tf_op jit(solution)/shard_map/all_gather | solution.py:118
  802.3 98.7 %copy-start.3 = (bf16[4,32,144]{1,0,2:T(4,128)(2,1)}, bf16[4,32,144]{1,0,2:T(4,128)(2,1)S(1)}, u32[]{:S(2)}) copy-start(bf16[4,32,144]{1,0,2:T(4,128)(2,1)S(1)} %add_convert_fusion.2) | copy-start | bytes 110596
  802.3 5.9 collective-permute-start.1
  809.1 304.1 %reduce-scatter.17.cloned.1.call-start = ((), (), s32[]{:S(2)}) async-start(), calls=%async_computation.14 | async-start | bytes 1216512
  901.0 1.0 copy-start.11
  916.0 291.0 %all-gather.15.cloned.1.call-start = ((), (), s32[]{:S(2)}) async-start(), calls=%async_computation.7 | async-start | bytes 4866048 | tf_op jit(solution)/shard_map/all_gather | solution.py:118
  1114.3 98.7 %copy-start.5 = (bf16[4,32,144]{1,0,2:T(4,128)(2,1)}, bf16[4,32,144]{1,0,2:T(4,128)(2,1)S(1)}, u32[]{:S(2)}) copy-start(bf16[4,32,144]{1,0,2:T(4,128)(2,1)S(1)} %add_convert_fusion.1) | copy-start | bytes 110596
  1114.3 5.9 collective-permute-start.2
  1121.1 304.2 %reduce-scatter.19.cloned.1.call-start = ((), (), s32[]{:S(2)}) async-start(), calls=%async_computation.15 | async-start | bytes 1216512
  1213.0 1.1 copy-start.13
  1221.5 9.2 copy-start.23
  1221.5 9.2 copy-start.17
  1221.5 204.7 %copy-start.4 = (bf16[4,32,144]{1,0,2:T(4,128)(2,1)S(1)}, bf16[4,32,144]{1,0,2:T(4,128)(2,1)}, u32[]{:S(2)}) copy-start(bf16[4,32,144]{1,0,2:T(4,128)(2,1)} %copy-done.3) | copy-start | bytes 110596
  1221.5 204.7 %copy-start.6 = (bf16[4,32,144]{1,0,2:T(4,128)(2,1)S(1)}, bf16[4,32,144]{1,0,2:T(4,128)(2,1)}, u32[]{:S(2)}) copy-start(bf16[4,32,144]{1,0,2:T(4,128)(2,1)} %copy-done.5) | copy-start | bytes 110596
  1228.0 284.5 %all-gather.23.cloned.1.call-start = ((), (), s32[]{:S(2)}) async-start(), calls=%async_computation.11 | async-start | bytes 4866048 | tf_op jit(solution)/shard_map/all_gather | solution.py:133
  1228.6 367.7 %all-gather.21.cloned.1.call-start = ((), (), s32[]{:S(2)}) async-start(), calls=%async_computation.10 | async-start | bytes 4866048 | tf_op jit(solution)/shard_map/all_gather | solution.py:133
  1229.3 450.6 %all-gather.19.cloned.1.call-start = ((), (), s32[]{:S(2)}) async-start(), calls=%async_computation.9 | async-start | bytes 4866048 | tf_op jit(solution)/shard_map/all_gather | solution.py:133
  1229.9 533.7 %all-gather.17.cloned.1.call-start = ((), (), s32[]{:S(2)}) async-start(), calls=%async_computation.8 | async-start | bytes 4866048 | tf_op jit(solution)/shard_map/all_gather | solution.py:133
  1427.3 89.8 %copy-start.8 = (bf16[4,32,4608]{2,1,0:T(8,128)(2,1)S(1)}, bf16[4,32,4608]{2,1,0:T(8,128)(2,1)}, u32[]{:S(2)}) copy-start(bf16[4,32,4608]{2,1,0:T(8,128)(2,1)} %copy-done.7) | copy-start | bytes 3538948
  1532.0 68.8 %copy-start.10 = (bf16[4,32,4608]{2,1,0:T(8,128)(2,1)S(1)}, bf16[4,32,4608]{2,1,0:T(8,128)(2,1)}, u32[]{:S(2)}) copy-start(bf16[4,32,4608]{2,1,0:T(8,128)(2,1)} %copy-done.9) | copy-start | bytes 3538948
  1615.7 68.7 %copy-start.12 = (bf16[4,32,4608]{2,1,0:T(8,128)(2,1)S(1)}, bf16[4,32,4608]{2,1,0:T(8,128)(2,1)}, u32[]{:S(2)}) copy-start(bf16[4,32,4608]{2,1,0:T(8,128)(2,1)} %copy-done.11) | copy-start | bytes 3538948
  1700.2 67.9 %copy-start.14 = (bf16[4,32,4608]{2,1,0:T(8,128)(2,1)S(1)}, bf16[4,32,4608]{2,1,0:T(8,128)(2,1)}, u32[]{:S(2)}) copy-start(bf16[4,32,4608]{2,1,0:T(8,128)(2,1)} %copy-done.13) | copy-start | bytes 3538948
  1783.1 9.4 copy-start.1
  1786.8 5.0 copy-start.20
Sparse Core Ops, SparseCore 0:
  11.5 179.0 all-reduce.2
  193.6 77.9 all-gather.8
  292.1 197.0 reduce-scatter.12
  497.2 85.6 all-gather.10
  604.0 197.1 reduce-scatter.14
  809.2 85.7 all-gather.12
  916.1 197.0 reduce-scatter.16
  1121.2 85.6 all-gather.14
  1228.1 197.1 reduce-scatter.18
  1428.0 84.4 all-gather.22
  1515.5 80.7 all-gather.20
  1599.1 80.7 all-gather.18
  1682.8 80.7 all-gather.16
where the time goes:
time: 1800 us
  waiting for transfers between devices  1590 us (88%)
  local copies, waits for them, and re-layouts  137 us (8%)
  matrix products  38.1 us (2%)
    unnamed x18, waiting for transfers between devices  964 us
    all_gather x4, waiting for transfers between devices, body(): full_in = lax.all_gather(current, 'feat', axis=2, tiled=True)  336 us
    all_gather x4, waiting for transfers between devices, body(): full_out = lax.all_gather(part_out, 'feat', axis=2, tiled=True)  277 us
    unnamed x62, local copies, waits for them, and re-layouts  54.6 us
    gather x4, local copies, waits for them, and re-layouts, feature_scores(): jnp.take(flat_scores, flat_index, axis=1)  39 us
  transfers between devices with their start and end apart: 16, of which 16 were waited for; matrix products, arithmetic and copies ran while one was open for 4% of the time, Pallas kernels for 0%

commit v1 on v0

v1 whole, which is shorter than its diff:
```python
import functools

import jax
import jax.numpy as jnp
from jax import lax
from jax.experimental import pallas as pl
from jax.experimental.pallas import tpu as pltpu
from jax.sharding import PartitionSpec as P

MESH = pl.DeviceIdType.MESH
F32 = jnp.float32
BF16 = jnp.bfloat16
NT = (((1,), (1,)), ((), ()))
TN = (((0,), (0,)), ((), ()))

D, HD, SEQ, FEATS, TGT = 4608, 128, 32, 32, 4
NZ, NY = 8, 4
SL = D // FEATS
COLS = TGT * SEQ
QUARTER = D // NY
PIECE = 640
STEP = QUARTER - PIECE
Z_ORDER = (1, 7, 2, 6, 3, 5, 4)
Y_ORDER = (1, 3, 2)


def main_kernel(
    ids_ref, pos_ref, tgain_ref, tscale_ref, pgain_ref, pscale_ref, qgain_ref, qscale_ref, pattern_ref,
    enc_hbm, out_hbm, val_hbm, dec_hbm,
    score_ref, grad_ref,
    enc, outp, val, dec, rows, e1, e2, e3, e2src, msg, recv, gslice, qslice,
    vt, full_in, full_mix, full_out,
    load_sem, e_send, e_recv, p_send, p_recv, v_send, v_recv, g_send, g_recv, x_send, x_recv,
):
    s = lax.axis_index("section")
    f = lax.axis_index("feat")
    c = lax.axis_index("row")
    z = f // NY
    y = f % NY

    def zdev(dz):
        return (s, lax.rem(z + dz, NZ) * NY + y, c)

    def ydev(dy):
        return (s, z * NY + lax.rem(y + dy, NY), c)

    def fdev(k):
        return (s, lax.rem(f + k, FEATS), c)

    def ycdev(k):
        j = lax.rem(y * 2 + c + k, 8)
        return (s, z * NY + j // 2, j % 2)

    def remote(src, dst, ss, rs, dev):
        return pltpu.make_async_remote_copy(
            src_ref=src, dst_ref=dst, send_sem=ss, recv_sem=rs, device_id=dev, device_id_type=MESH
        )

    load_enc = pltpu.make_async_copy(enc_hbm, enc, load_sem.at[0])
    load_out = pltpu.make_async_copy(out_hbm.at[0, 0], outp, load_sem.at[1])
    load_val = pltpu.make_async_copy(val_hbm.at[0, 0], val, load_sem.at[2])
    load_dec = pltpu.make_async_copy(dec_hbm.at[0], dec, load_sem.at[3])

    barrier = pltpu.get_barrier_semaphore()

    def greet(k, carry):
        pl.semaphore_signal(barrier, inc=1, device_id=fdev(k), device_id_type=MESH)
        return carry

    lax.fori_loop(1, FEATS, greet, 0)

    @pl.when(s == 3)
    def _():
        load_enc.start()

        def greet_cross(k, carry):
            j = lax.rem(y + k, NY)
            pl.semaphore_signal(barrier, inc=1, device_id=(s, z * NY + j, 1 - c), device_id_type=MESH)
            return carry

        lax.fori_loop(0, NY, greet_cross, 0)

    @pl.when(s < 3)
    def _():
        pl.semaphore_signal(barrier, inc=1, device_id=(s + 1, f, c), device_id_type=MESH)

    load_out.start()
    load_val.start()
    load_dec.start()

    lane_t = lax.broadcasted_iota(jnp.int32, (8, COLS), 1) // SEQ
    lane_p = lax.broadcasted_iota(jnp.int32, (8, COLS), 1) % SEQ
    row_t = lax.broadcasted_iota(jnp.int32, (8, COLS), 0)

    pattern4 = jnp.concatenate([pattern_ref[0, 0].astype(F32)] * TGT, axis=1)
    pscale4 = jnp.concatenate([pscale_ref[...]] * TGT, axis=1)
    qscale4 = jnp.concatenate([qscale_ref[...]] * TGT, axis=1)

    def column_of(gain_ref):
        for k in range(FEATS):
            qslice[k] = gain_ref[:, k * SL:(k + 1) * SL]
        row = qslice[f]
        eye = lax.broadcasted_iota(jnp.int32, (SL, SL), 0) == lax.broadcasted_iota(jnp.int32, (SL, SL), 1)
        return jnp.sum(jnp.where(eye, jnp.broadcast_to(row, (SL, SL)), 0.0), axis=1, keepdims=True)

    def gather_start(full, blk, k):
        def copy(b, dev, i):
            part = full.at[pl.ds(pl.multiple_of(b * blk, 16), blk)]
            return remote(part, part, g_send.at[k, i], g_recv.at[k, b], dev)

        sent = []
        for i, dy in enumerate(Y_ORDER):
            sent.append(copy(f, ydev(dy), i))
            sent[-1].start()
        for i, dz in enumerate(Z_ORDER):
            sent.append(copy(f, zdev(dz), 3 + i))
            sent[-1].start()
        for i, dz in enumerate(Z_ORDER):
            b = lax.rem(z + NZ - dz, NZ) * NY + y
            copy(b, zdev(0), 3 + i).wait_recv()
            for j, dy in enumerate(Y_ORDER):
                sent.append(copy(b, ydev(dy), 10 + 3 * i + j))
                sent[-1].start()
        return sent, copy

    def gather(full, blk, k):
        sent, copy = gather_start(full, blk, k)
        for dz in (0,) + Z_ORDER:
            for dy in Y_ORDER:
                b = lax.rem(z + NZ - dz, NZ) * NY + lax.rem(y + dy, NY)
                copy(b, ydev(1), 0).wait_recv()
        return sent

    def finish(sent):
        for item in sent:
            item.wait_send()

    own = pl.ds(pl.multiple_of(f * SL, 16), SL)
    own_head = pl.ds(pl.multiple_of(f * HD, 128), HD)

    def pass_down(block_src):
        return remote(block_src, full_in.at[own], x_send, x_recv, (lax.rem(s + 3, 4), f, c))

    @pl.when(s == 3)
    def _():
        load_enc.wait()
        base = (f * 2 + c) * enc.shape[0]
        wanted = jnp.full((8, 1), -1, jnp.int32)
        for t in range(8):
            wanted = jnp.where(lax.broadcasted_iota(jnp.int32, (8, 1), 0) == t, ids_ref[t] - base, wanted)
        hit = lax.broadcasted_iota(jnp.int32, (8, enc.shape[0]), 1) == wanted
        rows[...] = jnp.dot(hit.astype(BF16), enc[...], preferred_element_type=F32)

        pl.semaphore_wait(barrier, FEATS + NY)

        me = y * 2 + c

        def e_copy(stage, src, dst, k, slot, dev):
            return remote(src, dst.at[slot], e_send.at[stage, k], e_recv.at[stage, slot], dev)

        def piece_of(j):
            return rows.at[:, pl.ds(pl.multiple_of((j // 2) * QUARTER + (j % 2) * STEP, 128), PIECE)]

        def e1_copy(k):
            return e_copy(0, piece_of(lax.rem(me + k, 8)), e1, k, me, ycdev(k))

        for k in range(1, 8):
            e1_copy(k).start()
        e1[me] = piece_of(me)[...]
        for k in range(1, 8):
            j = lax.rem(me + k, 8)
            e_copy(0, e2src, e1, 0, j, ycdev(1)).wait_recv()
        total = e1[0]
        for k in range(1, 8):
            total = total + e1[k]
        e2src[...] = total

        def e2_copy(dz):
            return e_copy(1, e2src, e2, dz, z, zdev(dz))

        for dz in Z_ORDER:
            e2_copy(dz).start()
        e2[z] = total
        for dz in Z_ORDER:
            e_copy(1, e2src, e2, 0, lax.rem(z + dz, NZ), zdev(1)).wait_recv()
        total = e2[0]
        for k in range(1, 8):
            total = total + e2[k]
        e3[me] = total

        def e3_copy(k):
            return e_copy(2, e3.at[me], e3, k, me, ycdev(k))

        for k in range(1, 8):
            e3_copy(k).start()
        for k in range(1, 8):
            j = lax.rem(me + k, 8)
            e_copy(2, e2src, e3, 0, j, ycdev(1)).wait_recv()
        pieces = []
        for k in range(NY):
            pieces.append(e3[2 * k])
            pieces.append(e3[2 * k + 1][:, PIECE - STEP:])
        raw = jnp.concatenate(pieces, axis=1)
        raw = jnp.where(c == 0, raw, pltpu.roll(raw, 4, 0))
        own_row = lax.broadcasted_iota(jnp.int32, (8, 1), 0)
        raw = jnp.where(own_row < TGT, raw, 0.0)

        at = jnp.full((8, 1), -1, jnp.int32)
        for t in range(TGT):
            at = jnp.where(own_row == t, jnp.where(c == 0, pos_ref[t], pos_ref[t + TGT]), at)
        at_pos = lax.broadcasted_iota(jnp.int32, (8, SEQ), 1) == at
        t_scale = jnp.sum(jnp.where(at_pos, jnp.broadcast_to(tscale_ref[...], (8, SEQ)), 0.0), axis=1, keepdims=True)
        p_scale = jnp.sum(jnp.where(at_pos, jnp.broadcast_to(pscale_ref[...], (8, SEQ)), 0.0), axis=1, keepdims=True)
        top = (raw * tgain_ref[...] * t_scale).astype(BF16)
        scaled = (top.astype(F32) * pgain_ref[...] * p_scale).astype(BF16)
        for k in range(1, 8):
            e1_copy(k).wait_send()
        rows[...] = top.astype(F32)
        load_out.wait()
        head_in = lax.dot_general(scaled, outp[...], NT, preferred_element_type=F32).astype(BF16)
        at_row = jnp.dot(at_pos.astype(BF16), pattern4.astype(BF16), preferred_element_type=F32)
        at_row = jnp.where(lane_t == row_t, at_row * qscale4, 0.0)
        load_val.wait()
        gap = jnp.zeros((SEQ - (SL - HD), HD), BF16)
        for k in range(FEATS):
            tail = val[k * SL + HD:(k + 1) * SL, :]
            weights = jnp.concatenate([val[k * SL:k * SL + HD, :]] + [tail, gap] * TGT, axis=0)
            out = lax.dot_general(head_in, weights, NT, preferred_element_type=F32)
            spread = jnp.where(lane_t == (row_t + 1) % TGT, out[:, HD:], 0.0)
            low = pltpu.roll(spread + at_row, 4, 0)
            msg[k] = jnp.where(row_t < TGT, out[:, :HD], low)

        def m_copy(k):
            return remote(msg.at[lax.rem(f + k, FEATS)], recv.at[f], p_send.at[k], p_recv.at[f], fdev(k))

        def m_start(k, carry):
            m_copy(k).start()
            return carry

        lax.fori_loop(1, FEATS, m_start, 0)
        recv[f] = msg[f]
        column = column_of(qgain_ref)
        for k in range(FEATS):
            gslice[k] = rows[:, k * SL:(k + 1) * SL]
        top_own = gslice[f].astype(BF16)
        at_lane = ((lane_t == row_t) & (lane_p == at)).astype(BF16)
        base_grad = lax.dot_general(top_own, at_lane, TN, preferred_element_type=F32)
        load_dec.wait()
        top_scores = lax.dot_general(dec[1], rows[...].astype(BF16), NT, preferred_element_type=F32)
        top_part = jnp.dot(top_scores, at_lane.astype(F32), preferred_element_type=F32,
                           precision=lax.Precision.HIGHEST)

        def m_wait(k, carry):
            j = lax.rem(f + k, FEATS)
            remote(msg.at[0], recv.at[j], p_send.at[0], p_recv.at[j], fdev(1)).wait_recv()
            return carry

        lax.fori_loop(1, FEATS, m_wait, 0)
        got = recv[...].reshape(FEATS * 8, COLS)
        got_row = lax.broadcasted_iota(jnp.int32, got.shape, 0) % 8
        got_t = lax.broadcasted_iota(jnp.int32, got.shape, 1) // SEQ
        low = jnp.where((got_row >= TGT) & (got_t == got_row - TGT), got, 0.0)
        high = pltpu.roll(low, FEATS * 8 - TGT, 0)
        left = got.astype(BF16)
        upper = lax.dot_general(left, high.astype(BF16), TN, preferred_element_type=F32)
        under = lax.dot_general(left, low.astype(BF16), TN, preferred_element_type=F32)
        tail_t = lax.broadcasted_iota(jnp.int32, (SL - HD, COLS), 1) // SEQ
        tail = jnp.zeros((SL - HD, COLS), F32)
        for t in range(TGT):
            start = SEQ * ((t + 1) % TGT)
            tail = tail + jnp.where(tail_t == t, under[start:start + SL - HD, :], 0.0)
        new = base_grad + jnp.concatenate([upper, tail], axis=0) * column
        grad_ref[...] = new.astype(BF16).astype(F32)
        full_out[own, :] = new.astype(BF16)
        down = pass_down(full_out.at[own])
        down.start()
        sent = gather(full_out, SL, 2)
        score_ref[...] = top_part + jnp.dot(dec[0], full_out[...], preferred_element_type=F32)
        for k in range(1, 8):
            e3_copy(k).wait_send()
        for dz in Z_ORDER:
            e2_copy(dz).wait_send()

        def m_done(k, carry):
            m_copy(k).wait_send()
            return carry

        lax.fori_loop(1, FEATS, m_done, 0)
        down.wait_send()
        finish(sent)

    @pl.when(s < 3)
    def _():
        @pl.when(s > 0)
        def _():
            pl.semaphore_wait(barrier, FEATS)

        @pl.when(s == 0)
        def _():
            pl.semaphore_wait(barrier, FEATS - 1)

        load_val.wait()

        def v_copy(k):
            j = lax.rem(f + k, FEATS)
            return remote(val.at[pl.ds(pl.multiple_of(j * SL, 16), SL)], vt.at[:, own_head],
                          v_send.at[k], v_recv.at[f], fdev(k))

        def v_start(k, carry):
            v_copy(k).start()
            return carry

        lax.fori_loop(1, FEATS, v_start, 0)
        vt[:, own_head] = val[own, :]
        column = column_of(qgain_ref)
        load_out.wait()
        outp[...] = (outp[...].astype(F32) * pgain_ref[...]).astype(BF16)
        mixer = jnp.concatenate([pattern4] * TGT, axis=0)
        mix_q = lax.broadcasted_iota(jnp.int32, mixer.shape, 0) // SEQ
        mix_p = lax.broadcasted_iota(jnp.int32, mixer.shape, 1) // SEQ
        mixer = jnp.where(mix_q == mix_p, mixer, 0.0).astype(BF16)
        load_dec.wait()

        def v_wait(k, carry):
            j = lax.rem(f + k, FEATS)
            part = pl.ds(pl.multiple_of(j * HD, 128), HD)
            remote(val.at[own], vt.at[:, part], v_send.at[0], v_recv.at[j], fdev(1)).wait_recv()
            return carry

        lax.fori_loop(1, FEATS, v_wait, 0)

        def v_done(k, carry):
            v_copy(k).wait_send()
            return carry

        lax.fori_loop(1, FEATS, v_done, 0)

        pass_down(full_out.at[own]).wait_recv()
        sent = gather(full_in, SL, 0)
        head_in = jnp.dot(outp[...], full_in[...], preferred_element_type=F32)
        head_in = (head_in * pscale4).astype(BF16)
        head_mix = jnp.dot(head_in, mixer, preferred_element_type=F32) * qscale4
        full_mix[own_head, :] = head_mix.astype(BF16)
        sent = sent + gather(full_mix, HD, 1)
        new = jnp.dot(vt[...], full_mix[...], preferred_element_type=F32) * column
        new = new + full_in[own, :].astype(F32)
        grad_ref[...] = new.astype(BF16).astype(F32)
        full_out[own, :] = new.astype(BF16)
        down = pass_down(full_out.at[own])

        @pl.when(s > 0)
        def _():
            down.start()

        part_scores = jnp.dot(dec[1], full_in[...], preferred_element_type=F32)
        score_ref[...] = part_scores
        sent = sent + gather(full_out, SL, 2)
        score_ref[...] += jnp.dot(dec[0], full_out[...], preferred_element_type=F32)

        @pl.when(s > 0)
        def _():
            down.wait_send()

        finish(sent)


def pick_kernel(pos_ref, count_ref, ids_ref, act_ref, score_ref, grad_ref, out_ref, grad_out_ref, turned, picked):
    turned[...] = score_ref[...].T
    grad_out_ref[0] = grad_ref[...].T.astype(BF16).reshape(TGT, SEQ, SL)
    slots, width = ids_ref.shape[1], ids_ref.shape[2]
    for b in range(slots):
        at = pos_ref[0, b]
        for t in range(TGT):
            picked[t, b:b + 1, :] = turned[pl.ds(t * SEQ + at, 1), :]
    ids = ids_ref[0]
    live = lax.broadcasted_iota(jnp.int32, (slots, width), 0) < count_ref[0, 0]
    inner = ids % 128
    for t in range(TGT):
        low = jnp.take_along_axis(picked[t, :, :128], inner, axis=1, mode="promise_in_bounds")
        high = jnp.take_along_axis(picked[t, :, 128:], inner, axis=1, mode="promise_in_bounds")
        value = jnp.where(ids < 128, low, high) * act_ref[0]
        out_ref[0, t] = jnp.where(live, value, 0.0)


def body(
    target_ids, target_pos, target_gain, target_scale, encoder, post_gain, post_scale, out_proj, pattern,
    value_proj, pre_gain, pre_scale, decoder, block_ids, block_pos, block_act, block_count,
):
    vmem = pl.BlockSpec(memory_space=pltpu.VMEM)
    smem = pl.BlockSpec(memory_space=pltpu.SMEM)
    hbm = pl.BlockSpec(memory_space=pl.ANY)
    dma = pltpu.SemaphoreType.DMA
    shard = encoder.shape[0]
    features = decoder.shape[2]
    scores, grads = pl.pallas_call(
        main_kernel,
        out_shape=(
            jax.ShapeDtypeStruct((features, COLS), F32),
            jax.ShapeDtypeStruct((SL, COLS), F32),
        ),
        in_specs=[smem, smem] + [vmem] * 7 + [hbm] * 4,
        out_specs=(vmem, vmem),
        scratch_shapes=[
            pltpu.VMEM((shard, D), BF16),
            pltpu.VMEM((HD, D), BF16),
            pltpu.VMEM((D, HD), BF16),
            pltpu.VMEM((2, features, D), BF16),
            pltpu.VMEM((8, D), F32),
            pltpu.VMEM((8, 8, PIECE), F32),
            pltpu.VMEM((8, 8, PIECE), F32),
            pltpu.VMEM((8, 8, PIECE), F32),
            pltpu.VMEM((8, PIECE), F32),
            pltpu.VMEM((FEATS, 8, COLS), F32),
            pltpu.VMEM((FEATS, 8, COLS), F32),
            pltpu.VMEM((FEATS, 8, SL), F32),
            pltpu.VMEM((FEATS, 1, SL), F32),
            pltpu.VMEM((SL, FEATS * HD), BF16),
            pltpu.VMEM((D, COLS), BF16),
            pltpu.VMEM((FEATS * HD, COLS), BF16),
            pltpu.VMEM((D, COLS), BF16),
            dma((4,)),
            dma((3, 8)),
            dma((3, 8)),
            dma((FEATS,)),
            dma((FEATS,)),
            dma((FEATS,)),
            dma((FEATS,)),
            dma((3, FEATS)),
            dma((3, FEATS)),
            dma,
            dma,
        ],
        compiler_params=pltpu.CompilerParams(
            collective_id=1, has_side_effects=True, vmem_limit_bytes=48 * 1024 * 1024
        ),
        name="chain",
    )(
        target_ids, target_pos, target_gain.reshape(1, D), target_scale.reshape(1, SEQ), post_gain, post_scale,
        pre_gain, pre_scale, pattern, encoder, out_proj, value_proj, decoder,
    )
    slots, width = block_ids.shape[1], block_ids.shape[2]
    return pl.pallas_call(
        pick_kernel,
        out_shape=(
            jax.ShapeDtypeStruct((1, TGT, slots, width), F32),
            jax.ShapeDtypeStruct((1, TGT, SEQ, SL), BF16),
        ),
        in_specs=[smem, smem] + [vmem] * 4,
        out_specs=(vmem, vmem),
        scratch_shapes=[pltpu.VMEM((COLS, features), F32), pltpu.VMEM((TGT, slots, features), F32)],
        name="pick",
    )(block_pos, block_count, block_ids, block_act, scores, grads)


def solution(mesh):
    in_specs = (
        P(),
        P(),
        P(),
        P(),
        P(("feat", "row"), None),
        P("section", None),
        P("section", None),
        P("section", "feat", None, None),
        P("section", "feat", None, None),
        P("section", "feat", None, None),
        P("section", None),
        P("section", None),
        P("section", None, "feat", None),
        P("section", "feat", None),
        P("section", "feat"),
        P("section", "feat", None),
        P("section", "feat"),
    )
    out_specs = (P("section", "row", "feat", None), P("section", "row", None, "feat"))
    return jax.shard_map(body, mesh=mesh, in_specs=in_specs, out_specs=out_specs, check_vma=False)
```

time: 1800 us -> 172 us (0.10)
  the two profiles are of different devices: /device:TPU:1 before, /device:TPU:32 now
where the time goes in v1:
time: 172 us
  Pallas kernels  159 us (92%)
  local copies, waits for them, and re-layouts  11.6 us (7%)
    pallas_call x1, Pallas kernels, body(): pl.pallas_call(main_kernel, out_shape=(jax.ShapeDtypeStruct((features, CO...  157 us
    unnamed x26, local copies, waits for them, and re-layouts  10.9 us

profile of v1, /device:TPU:32, one launch (start us, length us, event | category | flops | bytes accessed | tf_op | source)
XLA Modules:
  0.0 171.7 jit_solution(14608738614361271798)
XLA Ops:
  1.3 0.7 reshape.10.tgain_ref
  2.0 0.0 copy-start
  2.0 1.7 copy-done
  3.7 0.0 copy-start.1
  3.7 1.3 copy-done.1
  5.0 0.0 copy-start.2
  5.0 1.3 copy-done.2
  6.2 0.0 copy-start.5
  6.2 0.7 copy-done.5
  7.0 0.0 copy-start.6
  7.0 0.7 copy-done.6
  7.7 0.0 copy-start.7
  7.7 0.7 copy-done.7
  8.4 0.0 copy-start.8
  8.4 0.7 copy-done.8
  9.0 0.0 copy-start.9
  9.0 0.7 copy-done.9
  9.7 0.0 copy-start.10
  9.7 0.7 copy-done.10
  10.3 0.0 copy-start.11
  10.3 0.7 copy-done.11
  11.0 0.0 copy-start.12
  11.0 0.7 copy-done.12
  11.7 156.9 %chain.1 = (f32[256,128]{1,0:T(8,128)S(1)}, f32[144,128]{1,0:T(8,128)S(1)}) custom-call(s32[8]{0:T(128)S(1)} %copy-done.8, s32[8]{0:T(128)S(1)} %copy-done.9, f32[1,4608]{1,0:T(1,128)S(1)} %reshape.10.tgain_ref, f32[1,32]{1,0:T(1,128)S(1)} %bitcast.1, f32[1,4608]{1,0:T(1,128)S(1)} %copy-done.5, f32[1,32]{1,0:T(1,128)S(1)} %copy-done.11, ...), custom_call_target="tpu_custom_call" | custom-call | tf_op jit(solution)/shard_map/chain/pallas_call | solution.py:395
  168.5 0.0 copy-start.3
  168.6 0.6 copy-done.3
  169.2 0.0 copy-start.4
  169.2 0.6 copy-done.4
  169.8 1.9 %pick.1 = (f32[1,4,16,128]{3,2,1,0:T(8,128)}, bf16[1,4,32,144]{3,2,1,0:T(8,128)(2,1)}) custom-call(s32[1,16]{1,0:T(1,128)} %pos_ref.3, s32[1,1]{1,0:T(1,128)S(6)} %copy.19.count_ref, s32[1,16,128]{2,1,0:T(8,128)} %ids_ref.3, f32[1,16,128]{2,1,0:T(8,128)} %act_ref.1, f32[256,128]{1,0:T(8,128)} %copy-done.3, f32[144,128]{1,0:T(8,128)} %copy-done.4), custom_call_target="tpu_custom_call" | custom-call | tf_op jit(solution)/shard_map/pick/pallas_call | solution.py:442
Async XLA Ops:
  2.0 1.7 copy-start
  3.7 1.3 copy-start.1
  5.0 1.3 copy-start.2
  6.2 0.7 copy-start.5
  7.0 0.7 copy-start.6
  7.7 0.7 copy-start.7
  8.4 0.7 copy-start.8
  9.0 0.7 copy-start.9
  9.7 0.7 copy-start.10
  10.3 0.7 copy-start.11
  11.0 0.7 copy-start.12
  168.5 0.7 copy-start.3
  169.2 0.6 copy-start.4

commit v2 on v1

v2 whole, which is shorter than its diff:
```python
import functools

import jax
import jax.numpy as jnp
from jax import lax
from jax.experimental import pallas as pl
from jax.experimental.pallas import tpu as pltpu
from jax.sharding import PartitionSpec as P

MESH = pl.DeviceIdType.MESH
F32 = jnp.float32
BF16 = jnp.bfloat16
NT = (((1,), (1,)), ((), ()))
TN = (((0,), (0,)), ((), ()))

D, HD, SEQ, FEATS, TGT = 4608, 128, 32, 32, 4
NZ, NY = 8, 4
SL = D // FEATS
COLS = TGT * SEQ
QUARTER = D // NY
BLOCK = D // NZ
WIN = 640
PAD = WIN - BLOCK
Z_ORDER = (1, 7, 2, 6, 3, 5, 4)
Z_FAR = (4, 3, 5, 2, 6, 1, 7)
Y_ORDER = (1, 3, 2)
Y_FAR = (2, 1, 3)


def main_kernel(
    ids_hbm, pos_hbm, tgain_hbm, tscale_hbm, pgain_hbm, pscale_hbm, qgain_hbm, qscale_hbm, pattern_hbm,
    enc_hbm, out_hbm, val_hbm, dec_hbm,
    score_ref, grad_ref,
    ids_ref, pos_ref, tgain_ref, tscale_ref, pgain_ref, pscale_ref, qgain_ref, qscale_ref, pattern_ref,
    enc, outp, val, dec, rows, rows0, top_own, e1, e2, e3, e2src, msg, recv, gslice, qslice,
    ow, vw, mixw, gin, hsrc, hpart, hm, gsrc, gpart, res, up, out,
    load_sem, small_sem, core_sem, e_send, e_recv, p_send, p_recv, w_send, w_recv,
    gin_send, gin_recv, attr_send, h_send, h_recv, m_send, m_recv, y_send, y_recv, g_send, g_recv, go_sem,
):
    s = lax.axis_index("section")
    f = lax.axis_index("feat")
    c = lax.axis_index("row")
    z = f // NY
    y = f % NY

    def zdev(dz):
        return (s, lax.rem(z + dz, NZ) * NY + y, c)

    def ydev(dy):
        return (s, z * NY + lax.rem(y + dy, NY), c)

    def fdev(k):
        return (s, lax.rem(f + k, FEATS), c)

    def remote(src, dst, ss, rs, dev):
        return pltpu.make_async_remote_copy(
            src_ref=src, dst_ref=dst, send_sem=ss, recv_sem=rs, device_id=dev, device_id_type=MESH
        )

    load_enc = pltpu.make_async_copy(enc_hbm, enc, load_sem.at[0])
    load_out = pltpu.make_async_copy(out_hbm.at[0, 0], outp, load_sem.at[1])
    load_val = pltpu.make_async_copy(val_hbm.at[0, 0], val, load_sem.at[2])
    load_dec = pltpu.make_async_copy(dec_hbm.at[0], dec, load_sem.at[3])
    small = ((ids_hbm, ids_ref), (pos_hbm, pos_ref), (tgain_hbm, tgain_ref), (tscale_hbm, tscale_ref),
             (pgain_hbm, pgain_ref), (pscale_hbm, pscale_ref), (qgain_hbm, qgain_ref), (qscale_hbm, qscale_ref),
             (pattern_hbm, pattern_ref))
    small = [pltpu.make_async_copy(src, dst, small_sem.at[i]) for i, (src, dst) in enumerate(small)]

    @pl.when(s == 3)
    def _():
        load_enc.start()

    for item in small:
        item.start()
    load_out.start()
    load_val.start()
    load_dec.start()

    barrier = pltpu.get_barrier_semaphore()

    def hello(dev):
        pl.semaphore_signal(barrier, inc=1, device_id=dev, device_id_type=MESH)

    @pl.when(c == 0)
    def _():
        for dz in Z_ORDER:
            hello(zdev(dz))
        for dy in Y_ORDER:
            hello(ydev(dy))

    @pl.when(c == 1)
    def _():
        for dz in Z_ORDER:
            hello(zdev(dz))
        for dy in Y_ORDER:
            hello(ydev(dy))

        def other_planes(k, carry):
            q = lax.rem(s + k, 4)
            for dz in range(NZ):
                hello((q, lax.rem(z + dz, NZ) * NY + y, 1))
            for dy in Y_ORDER:
                hello((q, z * NY + lax.rem(y + dy, NY), 1))
            return carry

        lax.fori_loop(1, 4, other_planes, 0)

        @pl.when(s == 3)
        def _():
            def rest(dz, carry):
                for dy in Y_ORDER:
                    hello((s, lax.rem(z + dz, NZ) * NY + lax.rem(y + dy, NY), 1))
                return carry

            lax.fori_loop(1, NZ, rest, 0)

    for q in range(4):
        hello((q, f, 1 - c))
    for item in small:
        item.wait()

    lane_t = lax.broadcasted_iota(jnp.int32, (8, COLS), 1) // SEQ
    lane_p = lax.broadcasted_iota(jnp.int32, (8, COLS), 1) % SEQ
    row_t = lax.broadcasted_iota(jnp.int32, (8, COLS), 0)
    own_row = lax.broadcasted_iota(jnp.int32, (8, 1), 0)
    own = pl.ds(pl.multiple_of(f * SL, 16), SL)
    gin_own = pl.ds(pl.multiple_of(PAD + y * SL, 16), SL)
    pattern = pattern_ref[0, 0].astype(F32)

    def column(row):
        n = row.shape[1]
        eye = lax.broadcasted_iota(jnp.int32, (n, n), 0) == lax.broadcasted_iota(jnp.int32, (n, n), 1)
        return jnp.sum(jnp.where(eye, jnp.broadcast_to(row, (n, n)), 0.0), axis=1, keepdims=True)

    def pick_rows():
        load_enc.wait()
        base = (f * 2 + c) * enc.shape[0]
        wanted = jnp.full((8, 1), -1, jnp.int32)
        for t in range(8):
            wanted = jnp.where(own_row == t, ids_ref[t] - base, wanted)
        hit = lax.broadcasted_iota(jnp.int32, (8, enc.shape[0]), 1) == wanted
        rows[...] = jnp.dot(hit.astype(BF16), enc[...], preferred_element_type=F32)

    def positions(group):
        at = jnp.full((8, 1), -1, jnp.int32)
        for t in range(TGT):
            at = jnp.where(own_row == t, pos_ref[t + TGT * group], at)
        return at

    def top_scores(group):
        at_lane = ((lane_t == row_t) & (lane_p == positions(group))).astype(F32)
        part = lax.dot_general(dec[1], top_own[...].astype(BF16), NT, preferred_element_type=F32)
        score_ref[...] = jnp.dot(part, at_lane, preferred_element_type=F32, precision=lax.Precision.HIGHEST)

    def gather(full, k, sent, use, arrives=True):
        def copy(b, dev, i):
            part = full.at[pl.ds(pl.multiple_of(b * SL, 16), SL)]
            return remote(part, part, g_send.at[k, i], g_recv.at[k, b], dev)

        def start(item):
            item.start()
            sent.append(item)

        def forward(b, i):
            for j, dy in enumerate(Y_ORDER):
                start(copy(b, ydev(dy), 3 * i + j))

        if arrives:
            copy(f, ydev(1), 0).wait_recv()
        forward(f, 0)
        for i, dz in enumerate(Z_ORDER):
            start(copy(f, zdev(dz), 24 + i))
        for i, dz in enumerate(Z_ORDER):
            b = lax.rem(z + NZ - dz, NZ) * NY + y
            copy(b, ydev(1), 0).wait_recv()
            forward(b, 1 + i)
        span = 2 * NY * SL
        for dq in (0, 1, 3, 2):
            q = lax.rem(z // 2 + dq, NZ // 2)
            for half in range(2):
                for dy in Y_ORDER:
                    b = (2 * q + half) * NY + lax.rem(y + dy, NY)
                    copy(b, ydev(1), 0).wait_recv()
            part = pl.ds(pl.multiple_of(q * span, 128), span)
            use(part, full[part, :])

    def add_up(part, block):
        score_ref[...] += jnp.dot(dec[1, :, part], block, preferred_element_type=F32)

    def add_out(part, block):
        score_ref[...] += jnp.dot(dec[0, :, part], block, preferred_element_type=F32)

    def finish(sent):
        for item in sent:
            item.wait_send()

    def attribution_copy(src, full, k, layer, group, i):
        return remote(src, full.at[own], attr_send.at[i], g_recv.at[k, f], (layer, f, group))

    def gin_copy(src, plane, dy, i, j):
        dev = (plane, z * NY + lax.rem(y + dy, NY), 1)
        return remote(src, gin.at[i, gin_own], gin_send.at[j, dy], gin_recv.at[i, y], dev)

    def gin_wait(i, dy):
        j = lax.rem(y + dy, NY)
        part = gin.at[i, pl.ds(pl.multiple_of(PAD + j * SL, 16), SL)]
        remote(part, part, gin_send.at[0, 0], gin_recv.at[i, j], ydev(1)).wait_recv()

    def w_copies(dest, di, slot, dz, kind):
        zz = lax.rem(z + dz, NZ)
        dev = (dest, zz * NY + y, 1)
        ss, rs = w_send.at[di, kind, dz], w_recv.at[slot, kind, z]
        if kind == 0:
            first = pl.multiple_of(zz * BLOCK - PAD * (zz % 2), 128)
            return remote(outp.at[:, pl.ds(first, WIN)], ow.at[slot, z], ss, rs, dev)
        src = val.at[pl.ds(pl.multiple_of(zz * BLOCK, 16), BLOCK)]
        dst = vw.at[slot, :, pl.ds(pl.multiple_of(z * HD, 128), HD)]
        return remote(src, dst, ss, rs, dev)

    def mix_copy(dest, di, slot):
        return remote(mixw.at[2], mixw.at[slot], w_send.at[di, 2, 0], w_recv.at[slot, 2, 0], (dest, f, 1))

    dest0 = jnp.where(s == 1, 1, 2)
    dest1 = jnp.where(s == 1, 0, 3)
    w_slot = jnp.where(s == 0, 1, 0)

    def weights_start():
        load_out.wait()
        outp[...] = (outp[...].astype(F32) * pgain_ref[...]).astype(BF16)
        scaled = pattern * column(pscale_ref[...]) * qscale_ref[...]
        wide = jnp.concatenate([scaled] * TGT, axis=1)
        wide = jnp.concatenate([wide] * TGT, axis=0)
        same = (lax.broadcasted_iota(jnp.int32, wide.shape, 0) // SEQ
                == lax.broadcasted_iota(jnp.int32, wide.shape, 1) // SEQ)
        mixw[2] = jnp.where(same, wide, 0.0).astype(BF16)

        def both(kind):
            for dz in Z_FAR:
                w_copies(dest0, 0, w_slot, dz, kind).start()
                w_copies(dest1, 1, w_slot, dz, kind).start()
            w_copies(dest1, 1, w_slot, 0, kind).start()

            @pl.when(s == 0)
            def _():
                w_copies(dest0, 0, w_slot, 0, kind).start()

        both(0)
        mix_copy(dest1, 1, w_slot).start()

        @pl.when(s == 0)
        def _():
            mix_copy(dest0, 0, w_slot).start()

        @pl.when(s > 0)
        def _():
            mixw[0] = mixw[2]
            ow[0, z] = outp[:, pl.ds(pl.multiple_of(z * BLOCK - PAD * (z % 2), 128), WIN)]

        load_val.wait()
        for k in range(FEATS):
            part = slice(k * SL, (k + 1) * SL)
            val[part, :] = (val[part, :].astype(F32) * column(qgain_ref[:, part])).astype(BF16)
        both(1)

        @pl.when(s > 0)
        def _():
            vw[0, :, pl.ds(pl.multiple_of(z * HD, 128), HD)] = val[pl.ds(pl.multiple_of(z * BLOCK, 16), BLOCK), :]

    def weights_done():
        for kind in range(2):
            for dz in Z_FAR:
                w_copies(dest0, 0, w_slot, dz, kind).wait_send()
                w_copies(dest1, 1, w_slot, dz, kind).wait_send()
            w_copies(dest1, 1, w_slot, 0, kind).wait_send()

            @pl.when(s == 0)
            def _():
                w_copies(dest0, 0, w_slot, 0, kind).wait_send()

        mix_copy(dest1, 1, w_slot).wait_send()

        @pl.when(s == 0)
        def _():
            mix_copy(dest0, 0, w_slot).wait_send()

    def w_wait(i, kind, home):
        def one(dz):
            zz = lax.rem(z + dz, NZ)
            if kind == 0:
                part = ow.at[i, zz]
            else:
                part = vw.at[i, :, pl.ds(pl.multiple_of(zz * HD, 128), HD)]
            remote(part, part, w_send.at[0, 0, 0], w_recv.at[i, kind, zz], ydev(1)).wait_recv()

        for dz in Z_ORDER:
            one(dz)
        if i == 1:
            one(0)
        else:
            @pl.when(jnp.logical_not(home))
            def _():
                one(0)

    def m_wait(i, home):
        def one():
            remote(mixw.at[i], mixw.at[i], w_send.at[0, 0, 0], w_recv.at[i, 2, 0], ydev(1)).wait_recv()

        if i == 1:
            one()
        else:
            pl.when(jnp.logical_not(home))(one)

    def layer_step(i):
        home = (s == 1) | (s == 2)
        gin[i, 0:PAD] = jnp.zeros((PAD, COLS), BF16)
        gin[i, PAD + BLOCK:] = jnp.zeros((PAD, COLS), BF16)
        w_wait(i, 0, home)
        m_wait(i, home)
        for dy in Y_ORDER:
            gin_wait(i, dy)
        if i == 1:
            gin_wait(i, 0)
        else:
            @pl.when(s < 3)
            def _():
                gin_wait(i, 0)

        block = gin[i, pl.ds(pl.multiple_of(PAD * (1 - z % 2), 16), WIN), :]

        def h_copy(dz):
            zz = lax.rem(z + dz, NZ)
            return remote(hsrc.at[i, zz], hpart.at[i, z], h_send.at[i, dz], h_recv.at[i, z], zdev(dz))

        for dz in Z_FAR:
            zz = lax.rem(z + dz, NZ)
            hsrc[i, zz] = jnp.dot(ow[i, zz], block, preferred_element_type=F32).astype(BF16)
            h_copy(dz).start()
        total = jnp.dot(ow[i, z], block, preferred_element_type=F32)
        for dz in Z_ORDER:
            zz = lax.rem(z + dz, NZ)
            remote(hpart.at[i, zz], hpart.at[i, zz], h_send.at[i, 0], h_recv.at[i, zz], ydev(1)).wait_recv()
            total = total + hpart[i, zz].astype(F32)
        mixed = jnp.dot(total.astype(BF16), mixw[i], preferred_element_type=F32).astype(BF16)
        mine = pl.ds(pl.multiple_of(z * HD, 128), HD)
        hm[i, mine, :] = mixed

        def hm_copy(dz):
            return remote(hm.at[i, mine], hm.at[i, mine], m_send.at[i, dz], m_recv.at[i, z], zdev(dz))

        for dz in Z_FAR:
            hm_copy(dz).start()
        w_wait(i, 1, home)
        for dz in Z_ORDER:
            zz = lax.rem(z + dz, NZ)
            part = hm.at[i, pl.ds(pl.multiple_of(zz * HD, 128), HD)]
            remote(part, part, m_send.at[i, 0], m_recv.at[i, zz], ydev(1)).wait_recv()

        def g_part(dy):
            yy = lax.rem(y + dy, NY)
            weights = vw[i, pl.ds(pl.multiple_of(yy * SL, 16), SL), :]
            return jnp.dot(weights, hm[i], preferred_element_type=F32)

        def gp_copy(dy):
            yy = lax.rem(y + dy, NY)
            return remote(gsrc.at[i, yy], gpart.at[i, y], y_send.at[i, dy], y_recv.at[i, y], ydev(dy))

        for dy in Y_FAR:
            gsrc[i, lax.rem(y + dy, NY)] = g_part(dy).astype(BF16)
            gp_copy(dy).start()
        total = g_part(0) + gin[i, gin_own, :].astype(F32)
        for dy in Y_ORDER:
            yy = lax.rem(y + dy, NY)
            remote(gpart.at[i, yy], gpart.at[i, yy], y_send.at[i, 0], y_recv.at[i, yy], ydev(1)).wait_recv()
            total = total + gpart[i, yy].astype(F32)
        res[i] = total.astype(BF16)

        def done():
            for dz in Z_FAR:
                h_copy(dz).wait_send()
                hm_copy(dz).wait_send()
            for dy in Y_FAR:
                gp_copy(dy).wait_send()

        return done

    def top_layer():
        me = y

        def quarter(j):
            return rows.at[:, pl.ds(pl.multiple_of(j * QUARTER, 128), QUARTER)]

        def e_copy(stage, src, dst, k, slot, dev):
            return remote(src, dst.at[slot], e_send.at[stage, k], e_recv.at[stage, slot], dev)

        remote(rows0, rows0, core_sem.at[0], core_sem.at[1], (s, f, 0)).wait_recv()
        rows[...] = rows[...] + rows0[...]

        def e1_copy(dy):
            return e_copy(0, quarter(lax.rem(y + dy, NY)), e1, dy, me, ydev(dy))

        for dy in Y_FAR:
            e1_copy(dy).start()
        total = quarter(me)[...]
        for dy in Y_ORDER:
            j = lax.rem(y + dy, NY)
            e_copy(0, e2src, e1, 0, j, ydev(1)).wait_recv()
            total = total + e1[j]
        e2src[...] = total

        def e2_copy(dz):
            return e_copy(1, e2src, e2, dz, z, zdev(dz))

        for dz in Z_FAR:
            e2_copy(dz).start()
        for dz in Z_ORDER:
            j = lax.rem(z + dz, NZ)
            e_copy(1, e2src, e2, 0, j, ydev(1)).wait_recv()
            total = total + e2[j]
        e3[me] = total

        def e3_copy(dy):
            return e_copy(2, e3.at[me], e3, dy, me, ydev(dy))

        for dy in Y_FAR:
            e3_copy(dy).start()
        for dy in Y_ORDER:
            e_copy(2, e2src, e3, 0, lax.rem(y + dy, NY), ydev(1)).wait_recv()
        for dy in Y_FAR:
            e1_copy(dy).wait_send()
        raw = jnp.concatenate([e3[k] for k in range(NY)], axis=1)

        tops, scaled, at_rows, lanes = [], [], [], []
        pattern4 = jnp.concatenate([pattern] * TGT, axis=1)
        qscale4 = jnp.concatenate([qscale_ref[...]] * TGT, axis=1)
        for group in range(2):
            part = raw if group == 0 else pltpu.roll(raw, TGT, 0)
            part = jnp.where(own_row < TGT, part, 0.0)
            at = positions(group)
            at_pos = lax.broadcasted_iota(jnp.int32, (8, SEQ), 1) == at
            t_scale = jnp.sum(jnp.where(at_pos, jnp.broadcast_to(tscale_ref[...], (8, SEQ)), 0.0),
                              axis=1, keepdims=True)
            p_scale = jnp.sum(jnp.where(at_pos, jnp.broadcast_to(pscale_ref[...], (8, SEQ)), 0.0),
                              axis=1, keepdims=True)
            top = (part * tgain_ref[...] * t_scale).astype(BF16).astype(F32)
            tops.append(top)
            scaled.append(top * pgain_ref[...] * p_scale)
            at_row = jnp.dot(at_pos.astype(BF16), pattern4.astype(BF16), preferred_element_type=F32)
            at_rows.append(jnp.where(lane_t == row_t, at_row * qscale4, 0.0))
            lanes.append(((lane_t == row_t) & (lane_p == at)).astype(BF16))
        rows[...] = tops[0]
        top_copy = remote(rows, top_own, core_sem.at[0], core_sem.at[1], (s, f, 0))
        top_own[...] = tops[1]
        load_out.wait()
        both = jnp.concatenate(scaled, axis=0).astype(BF16)
        head_in = lax.dot_general(both, outp[...], NT, preferred_element_type=F32).astype(BF16)
        load_val.wait()
        gap = jnp.zeros((SEQ - (SL - HD), HD), BF16)

        def m_copy(k):
            return remote(msg.at[lax.rem(f + k, FEATS)], recv.at[f], p_send.at[k], p_recv.at[f], fdev(k))

        for k in range(FEATS):
            tail = val[k * SL + HD:(k + 1) * SL, :]
            weights = jnp.concatenate([val[k * SL:k * SL + HD, :]] + [tail, gap] * TGT, axis=0)
            got = lax.dot_general(head_in, weights, NT, preferred_element_type=F32)
            for group in range(2):
                part = got[8 * group:8 * group + 8]
                spread = jnp.where(lane_t == (row_t + 1) % TGT, part[:, HD:], 0.0)
                low = pltpu.roll(spread + at_rows[group], TGT, 0)
                msg[k, 8 * group:8 * group + 8] = jnp.where(row_t < TGT, part[:, :HD], low)

        def m_start(k, carry):
            m_copy(k).start()
            return carry

        lax.fori_loop(1, FEATS, m_start, 0)
        recv[f] = msg[f]
        top_copy.start()
        for k in range(FEATS):
            qslice[k] = qgain_ref[:, k * SL:(k + 1) * SL]
        gain = column(qslice[f])
        bases = []
        for group in range(2):
            for k in range(FEATS):
                gslice[k] = tops[group][:, k * SL:(k + 1) * SL]
            bases.append(lax.dot_general(gslice[f].astype(BF16), lanes[group], TN, preferred_element_type=F32))

        def m_wait_one(k, carry):
            j = lax.rem(f + k, FEATS)
            remote(msg.at[0], recv.at[j], p_send.at[0], p_recv.at[j], fdev(1)).wait_recv()
            return carry

        lax.fori_loop(1, FEATS, m_wait_one, 0)
        tail_t = lax.broadcasted_iota(jnp.int32, (SL - HD, COLS), 1) // SEQ
        for group in range(2):
            got = recv[:, 8 * group:8 * group + 8, :].reshape(FEATS * 8, COLS)
            got_row = lax.broadcasted_iota(jnp.int32, got.shape, 0) % 8
            got_t = lax.broadcasted_iota(jnp.int32, got.shape, 1) // SEQ
            low = jnp.where((got_row >= TGT) & (got_t == got_row - TGT), got, 0.0)
            high = pltpu.roll(low, FEATS * 8 - TGT, 0)
            left = got.astype(BF16)
            upper = lax.dot_general(left, high.astype(BF16), TN, preferred_element_type=F32)
            under = lax.dot_general(left, low.astype(BF16), TN, preferred_element_type=F32)
            tail = jnp.zeros((SL - HD, COLS), F32)
            for t in range(TGT):
                start = SEQ * ((t + 1) % TGT)
                tail = tail + jnp.where(tail_t == t, under[start:start + SL - HD, :], 0.0)
            new = bases[group] + jnp.concatenate([upper, tail], axis=0) * gain
            res[2 + group] = new.astype(BF16)
            if group == 0:
                for dy in (2, 1, 3, 0):
                    gin_copy(res.at[2], 2, dy, 0, 0).start()
            else:
                for dy in Y_FAR:
                    gin_copy(res.at[3], 3, dy, 0, 1).start()
                gin[0, gin_own, :] = res[3]
                out[own, :] = res[3]
        notes = [attribution_copy(res.at[2], out, 1, 3, 0, 0), attribution_copy(res.at[2], up, 0, 2, 0, 1),
                 attribution_copy(res.at[3], up, 0, 2, 1, 2)]
        for item in notes:
            item.start()

        def done():
            for dy in Y_FAR:
                e3_copy(dy).wait_send()
                gin_copy(res.at[3], 3, dy, 0, 1).wait_send()
            for dy in range(NY):
                gin_copy(res.at[2], 2, dy, 0, 0).wait_send()
            for dz in Z_FAR:
                e2_copy(dz).wait_send()
            top_copy.wait_send()
            for item in notes:
                item.wait_send()

            def m_done(k, carry):
                m_copy(k).wait_send()
                return carry

            lax.fori_loop(1, FEATS, m_done, 0)

        return done

    def release():
        pl.semaphore_signal(go_sem, inc=1, device_id=(s, f, 0), device_id_type=MESH)

    to_plane = 3 - s
    gin_slot = jnp.where(s >= 2, 0, 1)
    layer_now = jnp.where(s >= 2, 2, 1)
    group_now = jnp.where((s == 1) | (s == 2), 0, 1)

    def send_copies():
        items = [gin_copy(res.at[0], to_plane, dy, gin_slot, 2) for dy in (2, 1, 3, 0)]
        return items + [attribution_copy(res.at[0], out, 1, layer_now, group_now, 3)]

    def up_copy():
        return attribution_copy(res.at[0], up, 0, layer_now - 1, group_now, 4)

    def send_on(i):
        for item in send_copies():
            item.start()

        @pl.when(s > 0)
        def _():
            up_copy().start()

        @pl.when(s == 0)
        def _():
            up[own, :] = res[0]

    def send_done():
        for item in send_copies():
            item.wait_send()

        @pl.when(s > 0)
        def _():
            up_copy().wait_send()

    @pl.when(c == 0)
    def _():
        @pl.when(s == 3)
        def _():
            pick_rows()
            pl.semaphore_wait(barrier, 14)
            give = remote(rows, rows0, core_sem.at[0], core_sem.at[1], (s, f, 1))
            give.start()
            load_dec.wait()
            remote(rows, top_own, core_sem.at[0], core_sem.at[1], (s, f, 1)).wait_recv()
            top_scores(0)
            pl.semaphore_wait(go_sem, 1)
            give.wait_send()

        @pl.when(s < 3)
        def _():
            pl.semaphore_wait(barrier, 14)
            score_ref[...] = jnp.zeros_like(score_ref)
            load_dec.wait()
            sent = []
            pl.semaphore_wait(go_sem, 1)
            gather(up, 0, sent, add_up)
            pl.semaphore_wait(go_sem, 1)
            finish(sent)

        sent = []
        gather(out, 1, sent, add_out)
        grad_ref[...] = out[own, :].astype(F32)
        finish(sent)
        load_out.wait()
        load_val.wait()

    @pl.when(c == 1)
    def _():
        @pl.when(s == 3)
        def _():
            pick_rows()
            pl.semaphore_wait(barrier, 68)
            top_done = top_layer()
            load_dec.wait()
            step_done = layer_step(0)
            send_on(0)
            release()
            top_scores(1)
            sent = []
            gather(out, 1, sent, add_out, arrives=False)
            grad_ref[...] = out[own, :].astype(F32)
            top_done()
            step_done()
            finish(sent)

        @pl.when(s < 3)
        def _():
            pl.semaphore_wait(barrier, 47)
            weights_start()
            score_ref[...] = jnp.zeros_like(score_ref)
            load_dec.wait()
            step_done = layer_step(0)
            send_on(0)
            release()
            sent = []

            @pl.when(s > 0)
            def _():
                more = []
                gather(up, 0, more, add_up)
                finish(more)

            @pl.when(s == 0)
            def _():
                more = []
                gather(up, 0, more, add_up, arrives=False)
                finish(more)

            step_done()
            weights_done()

        @pl.when(s >= 2)
        def _():
            step_done = layer_step(1)
            last = attribution_copy(res.at[1], out, 1, 0, s - 2, 6)
            last.start()
            step_done()
            last.wait_send()

        @pl.when(s < 3)
        def _():
            release()
            sent = []
            gather(out, 1, sent, add_out)
            grad_ref[...] = out[own, :].astype(F32)
            finish(sent)

        send_done()


def pick_kernel(pos_hbm, count_hbm, ids_hbm, act_hbm, score_ref, grad_ref, out_ref, grad_out_ref,
                pos_ref, count_ref, ids_ref, act_ref, turned, picked, sem):
    pairs = ((pos_hbm, pos_ref), (count_hbm, count_ref), (ids_hbm, ids_ref), (act_hbm, act_ref))
    copies = [pltpu.make_async_copy(src, dst, sem.at[i]) for i, (src, dst) in enumerate(pairs)]
    for item in copies:
        item.start()
    turned[...] = score_ref[...].T
    grad_out_ref[0] = grad_ref[...].T.astype(BF16).reshape(TGT, SEQ, SL)
    for item in copies:
        item.wait()
    slots, width = ids_ref.shape[1], ids_ref.shape[2]
    for b in range(slots):
        at = pos_ref[0, b]
        for t in range(TGT):
            picked[t, b:b + 1, :] = turned[pl.ds(t * SEQ + at, 1), :]
    ids = ids_ref[0]
    live = lax.broadcasted_iota(jnp.int32, (slots, width), 0) < count_ref[0, 0]
    inner = ids % 128
    for t in range(TGT):
        low = jnp.take_along_axis(picked[t, :, :128], inner, axis=1, mode="promise_in_bounds")
        high = jnp.take_along_axis(picked[t, :, 128:], inner, axis=1, mode="promise_in_bounds")
        value = jnp.where(ids < 128, low, high) * act_ref[0]
        out_ref[0, t] = jnp.where(live, value, 0.0)


def body(
    target_ids, target_pos, target_gain, target_scale, encoder, post_gain, post_scale, out_proj, pattern,
    value_proj, pre_gain, pre_scale, decoder, block_ids, block_pos, block_act, block_count,
):
    vmem = pl.BlockSpec(memory_space=pltpu.VMEM)
    hbm = pl.BlockSpec(memory_space=pltpu.HBM)
    dma = pltpu.SemaphoreType.DMA
    shard = encoder.shape[0]
    features = decoder.shape[2]
    scores, grads = pl.pallas_call(
        main_kernel,
        out_shape=(
            jax.ShapeDtypeStruct((features, COLS), F32),
            jax.ShapeDtypeStruct((SL, COLS), F32),
        ),
        in_specs=[hbm] * 13,
        out_specs=(vmem, vmem),
        scratch_shapes=[
            pltpu.SMEM((2 * TGT,), jnp.int32),
            pltpu.SMEM((2 * TGT,), jnp.int32),
            pltpu.VMEM((1, D), F32),
            pltpu.VMEM((1, SEQ), F32),
            pltpu.VMEM((1, D), F32),
            pltpu.VMEM((1, SEQ), F32),
            pltpu.VMEM((1, D), F32),
            pltpu.VMEM((1, SEQ), F32),
            pltpu.VMEM((1, 1, SEQ, SEQ), BF16),
            pltpu.VMEM((shard, D), BF16),
            pltpu.VMEM((HD, D), BF16),
            pltpu.VMEM((D, HD), BF16),
            pltpu.VMEM((2, features, D), BF16),
            pltpu.VMEM((8, D), F32),
            pltpu.VMEM((8, D), F32),
            pltpu.VMEM((8, D), F32),
            pltpu.VMEM((NY, 8, QUARTER), F32),
            pltpu.VMEM((NZ, 8, QUARTER), F32),
            pltpu.VMEM((NY, 8, QUARTER), F32),
            pltpu.VMEM((8, QUARTER), F32),
            pltpu.VMEM((FEATS, 16, COLS), F32),
            pltpu.VMEM((FEATS, 16, COLS), F32),
            pltpu.VMEM((FEATS, 8, SL), F32),
            pltpu.VMEM((FEATS, 1, SL), F32),
            pltpu.VMEM((2, NZ, HD, WIN), BF16),
            pltpu.VMEM((2, BLOCK, NZ * HD), BF16),
            pltpu.VMEM((3, COLS, COLS), BF16),
            pltpu.VMEM((2, BLOCK + 2 * PAD, COLS), BF16),
            pltpu.VMEM((2, NZ, HD, COLS), BF16),
            pltpu.VMEM((2, NZ, HD, COLS), BF16),
            pltpu.VMEM((2, NZ * HD, COLS), BF16),
            pltpu.VMEM((2, NY, SL, COLS), BF16),
            pltpu.VMEM((2, NY, SL, COLS), BF16),
            pltpu.VMEM((4, SL, COLS), BF16),
            pltpu.VMEM((D, COLS), BF16),
            pltpu.VMEM((D, COLS), BF16),
            dma((4,)),
            dma((9,)),
            dma((2,)),
            dma((3, NZ)),
            dma((3, NZ)),
            dma((FEATS,)),
            dma((FEATS,)),
            dma((2, 3, NZ)),
            dma((2, 3, NZ)),
            dma((3, NY)),
            dma((2, NY)),
            dma((8,)),
            dma((2, NZ)),
            dma((2, NZ)),
            dma((2, NZ)),
            dma((2, NZ)),
            dma((2, NY)),
            dma((2, NY)),
            dma((2, FEATS)),
            dma((2, FEATS)),
            pltpu.SemaphoreType.REGULAR,
        ],
        compiler_params=pltpu.CompilerParams(
            collective_id=1, has_side_effects=True, vmem_limit_bytes=60 * 1024 * 1024
        ),
        name="chain",
    )(
        target_ids, target_pos, target_gain.reshape(1, D), target_scale.reshape(1, SEQ), post_gain, post_scale,
        pre_gain, pre_scale, pattern, encoder, out_proj, value_proj, decoder,
    )
    slots, width = block_ids.shape[1], block_ids.shape[2]
    return pl.pallas_call(
        pick_kernel,
        out_shape=(
            jax.ShapeDtypeStruct((1, TGT, slots, width), F32),
            jax.ShapeDtypeStruct((1, TGT, SEQ, SL), BF16),
        ),
        in_specs=[hbm] * 4 + [vmem] * 2,
        out_specs=(vmem, vmem),
        scratch_shapes=[
            pltpu.SMEM((1, slots), jnp.int32),
            pltpu.SMEM((1, 1), jnp.int32),
            pltpu.VMEM((1, slots, width), jnp.int32),
            pltpu.VMEM((1, slots, width), F32),
            pltpu.VMEM((COLS, features), F32),
            pltpu.VMEM((TGT, slots, features), F32),
            dma((4,)),
        ],
        name="pick",
    )(block_pos, block_count, block_ids, block_act, scores, grads)


def solution(mesh):
    in_specs = (
        P(),
        P(),
        P(),
        P(),
        P(("feat", "row"), None),
        P("section", None),
        P("section", None),
        P("section", "feat", None, None),
        P("section", "feat", None, None),
        P("section", "feat", None, None),
        P("section", None),
        P("section", None),
        P("section", None, "feat", None),
        P("section", "feat", None),
        P("section", "feat"),
        P("section", "feat", None),
        P("section", "feat"),
    )
    out_specs = (P("section", "row", "feat", None), P("section", "row", None, "feat"))
    return jax.shard_map(body, mesh=mesh, in_specs=in_specs, out_specs=out_specs, check_vma=False)
```

time: 172 us -> 142 us (0.83)
  the two profiles are of different devices: /device:TPU:32 before, /device:TPU:4 now
where the time goes in v2:
time: 142 us
  Pallas kernels  139 us (98%)
  between operations  1.47 us (1%)
    pallas_call x1, Pallas kernels, body(): pl.pallas_call(main_kernel, out_shape=(jax.ShapeDtypeStruct((features, CO...  136 us

profile of v2, /device:TPU:4, one launch (start us, length us, event | category | flops | bytes accessed | tf_op | source)
XLA Modules:
  0.0 141.7 jit_solution(5766695958990929609)
XLA Ops:
  1.3 1.3 reshape.10.tgain_hbm
  2.6 136.4 %chain.1 = (f32[256,128]{1,0:T(8,128)}, f32[144,128]{1,0:T(8,128)}) custom-call(s32[8]{0:T(128)} %ids_hbm.2, s32[8]{0:T(128)} %pos_hbm.2, f32[1,4608]{1,0:T(1,128)} %reshape.10.tgain_hbm, f32[1,32]{1,0:T(1,128)} %bitcast.1, f32[1,4608]{1,0:T(1,128)} %pgain_hbm.1, f32[1,32]{1,0:T(1,128)} %pscale_hbm.1, f32[1,4608]{1,0:T(1,128)} %qgain_hbm.1, ...), custom_call_target="tpu_custom_call" | custom-call | tf_op jit(solution)/shard_map/chain/pallas_call | solution.py:708
  139.1 2.5 %pick.1 = (f32[1,4,16,128]{3,2,1,0:T(8,128)}, bf16[1,4,32,144]{3,2,1,0:T(8,128)(2,1)}) custom-call(s32[1,16]{1,0:T(1,128)} %pos_hbm.3, s32[1,1]{1,0:T(1,128)S(6)} %copy.19.count_hbm, s32[1,16,128]{2,1,0:T(8,128)} %ids_hbm.3, f32[1,16,128]{2,1,0:T(8,128)} %act_hbm.1, f32[256,128]{1,0:T(8,128)} %get-tuple-element.4.score_ref, f32[144,128]{1,0:T(8,128)} %get-tuple-element.5.grad_ref), custom_call_target="tpu_custom_call" | custom-call | tf_op jit(solution)/shard_map/pick/pallas_call | solution.py:784

commit v3 on v2

--- a/solution.py
+++ b/solution.py
@@ -34,7 +34,7 @@
     ids_ref, pos_ref, tgain_ref, tscale_ref, pgain_ref, pscale_ref, qgain_ref, qscale_ref, pattern_ref,
     enc, outp, val, dec, rows, rows0, top_own, e1, e2, e3, e2src, msg, recv, gslice, qslice,
     ow, vw, mixw, gin, hsrc, hpart, hm, gsrc, gpart, res, up, out,
-    load_sem, small_sem, core_sem, e_send, e_recv, p_send, p_recv, w_send, w_recv,
+    load_sem, small_sem, core_sem, e_send, e_recv, p_send, p_recv, w_send, w_recv, f_send, f_recv,
     gin_send, gin_recv, attr_send, h_send, h_recv, m_send, m_recv, y_send, y_recv, g_send, g_recv, go_sem,
 ):
     s = lax.axis_index("section")
@@ -206,116 +206,90 @@
         part = gin.at[i, pl.ds(pl.multiple_of(PAD + j * SL, 16), SL)]
         remote(part, part, gin_send.at[0, 0], gin_recv.at[i, j], ydev(1)).wait_recv()
 
-    def w_copies(dest, di, slot, dz, kind):
+    home_slot = jnp.where(s == 0, 1, 0)
+
+    def w_copy(dz, kind):
         zz = lax.rem(z + dz, NZ)
-        dev = (dest, zz * NY + y, 1)
-        ss, rs = w_send.at[di, kind, dz], w_recv.at[slot, kind, z]
+        ss, rs = w_send.at[kind, dz], w_recv.at[kind, z]
         if kind == 0:
             first = pl.multiple_of(zz * BLOCK - PAD * (zz % 2), 128)
-            return remote(outp.at[:, pl.ds(first, WIN)], ow.at[slot, z], ss, rs, dev)
+            return remote(outp.at[:, pl.ds(first, WIN)], ow.at[home_slot, z], ss, rs, zdev(dz))
         src = val.at[pl.ds(pl.multiple_of(zz * BLOCK, 16), BLOCK)]
-        dst = vw.at[slot, :, pl.ds(pl.multiple_of(z * HD, 128), HD)]
-        return remote(src, dst, ss, rs, dev)
-
-    def mix_copy(dest, di, slot):
-        return remote(mixw.at[2], mixw.at[slot], w_send.at[di, 2, 0], w_recv.at[slot, 2, 0], (dest, f, 1))
-
-    dest0 = jnp.where(s == 1, 1, 2)
-    dest1 = jnp.where(s == 1, 0, 3)
-    w_slot = jnp.where(s == 0, 1, 0)
+        dst = vw.at[home_slot, :, pl.ds(pl.multiple_of(z * HD, 128), HD)]
+        return remote(src, dst, ss, rs, zdev(dz))
+
+    def on_copy(kind, di):
+        ref = (ow, vw, mixw)[kind].at[home_slot]
+        dest = 2 if di == 1 else jnp.where(s == 1, 0, 3)
+        return remote(ref, ref, f_send.at[di, kind], f_recv.at[home_slot, kind], (dest, f, 1))
+
+    def on_start(kind):
+        on_copy(kind, 0).start()
+
+        @pl.when(s == 0)
+        def _():
+            on_copy(kind, 1).start()
+
+    def w_arrived(kind):
+        for dz in Z_ORDER:
+            zz = lax.rem(z + dz, NZ)
+            if kind == 0:
+                part = ow.at[home_slot, zz]
+            else:
+                part = vw.at[home_slot, :, pl.ds(pl.multiple_of(zz * HD, 128), HD)]
+            remote(part, part, w_send.at[kind, 0], w_recv.at[kind, zz], ydev(1)).wait_recv()
 
     def weights_start():
         load_out.wait()
         outp[...] = (outp[...].astype(F32) * pgain_ref[...]).astype(BF16)
+        for dz in Z_FAR:
+            w_copy(dz, 0).start()
+        ow[home_slot, z] = outp[:, pl.ds(pl.multiple_of(z * BLOCK - PAD * (z % 2), 128), WIN)]
         scaled = pattern * column(pscale_ref[...]) * qscale_ref[...]
         wide = jnp.concatenate([scaled] * TGT, axis=1)
         wide = jnp.concatenate([wide] * TGT, axis=0)
         same = (lax.broadcasted_iota(jnp.int32, wide.shape, 0) // SEQ
                 == lax.broadcasted_iota(jnp.int32, wide.shape, 1) // SEQ)
-        mixw[2] = jnp.where(same, wide, 0.0).astype(BF16)
-
-        def both(kind):
-            for dz in Z_FAR:
-                w_copies(dest0, 0, w_slot, dz, kind).start()
-                w_copies(dest1, 1, w_slot, dz, kind).start()
-            w_copies(dest1, 1, w_slot, 0, kind).start()
-
-            @pl.when(s == 0)
-            def _():
-                w_copies(dest0, 0, w_slot, 0, kind).start()
-
-        both(0)
-        mix_copy(dest1, 1, w_slot).start()
-
-        @pl.when(s == 0)
-        def _():
-            mix_copy(dest0, 0, w_slot).start()
-
-        @pl.when(s > 0)
-        def _():
-            mixw[0] = mixw[2]
-            ow[0, z] = outp[:, pl.ds(pl.multiple_of(z * BLOCK - PAD * (z % 2), 128), WIN)]
-
+        mixw[home_slot] = jnp.where(same, wide, 0.0).astype(BF16)
+        on_start(2)
         load_val.wait()
         for k in range(FEATS):
             part = slice(k * SL, (k + 1) * SL)
             val[part, :] = (val[part, :].astype(F32) * column(qgain_ref[:, part])).astype(BF16)
-        both(1)
-
-        @pl.when(s > 0)
-        def _():
-            vw[0, :, pl.ds(pl.multiple_of(z * HD, 128), HD)] = val[pl.ds(pl.multiple_of(z * BLOCK, 16), BLOCK), :]
+        for dz in Z_FAR:
+            w_copy(dz, 1).start()
+        vw[home_slot, :, pl.ds(pl.multiple_of(z * HD, 128), HD)] = val[pl.ds(pl.multiple_of(z * BLOCK, 16), BLOCK), :]
+        w_arrived(0)
+        on_start(0)
+        w_arrived(1)
+        on_start(1)
 
     def weights_done():
         for kind in range(2):
             for dz in Z_FAR:
-                w_copies(dest0, 0, w_slot, dz, kind).wait_send()
-                w_copies(dest1, 1, w_slot, dz, kind).wait_send()
-            w_copies(dest1, 1, w_slot, 0, kind).wait_send()
+                w_copy(dz, kind).wait_send()
+        for kind in range(3):
+            on_copy(kind, 0).wait_send()
 
             @pl.when(s == 0)
             def _():
-                w_copies(dest0, 0, w_slot, 0, kind).wait_send()
-
-        mix_copy(dest1, 1, w_slot).wait_send()
-
-        @pl.when(s == 0)
-        def _():
-            mix_copy(dest0, 0, w_slot).wait_send()
-
-    def w_wait(i, kind, home):
-        def one(dz):
-            zz = lax.rem(z + dz, NZ)
-            if kind == 0:
-                part = ow.at[i, zz]
-            else:
-                part = vw.at[i, :, pl.ds(pl.multiple_of(zz * HD, 128), HD)]
-            remote(part, part, w_send.at[0, 0, 0], w_recv.at[i, kind, zz], ydev(1)).wait_recv()
-
-        for dz in Z_ORDER:
-            one(dz)
-        if i == 1:
-            one(0)
-        else:
-            @pl.when(jnp.logical_not(home))
-            def _():
-                one(0)
-
-    def m_wait(i, home):
+                on_copy(kind, 1).wait_send()
+
+    def w_wait(i, kind):
         def one():
-            remote(mixw.at[i], mixw.at[i], w_send.at[0, 0, 0], w_recv.at[i, 2, 0], ydev(1)).wait_recv()
+            ref = (ow, vw, mixw)[kind].at[i]
+            remote(ref, ref, f_send.at[0, kind], f_recv.at[i, kind], ydev(1)).wait_recv()
 
         if i == 1:
             one()
         else:
-            pl.when(jnp.logical_not(home))(one)
+            pl.when((s == 0) | (s == 3))(one)
 
     def layer_step(i):
-        home = (s == 1) | (s == 2)
         gin[i, 0:PAD] = jnp.zeros((PAD, COLS), BF16)
         gin[i, PAD + BLOCK:] = jnp.zeros((PAD, COLS), BF16)
-        w_wait(i, 0, home)
-        m_wait(i, home)
+        w_wait(i, 0)
+        w_wait(i, 2)
         for dy in Y_ORDER:
             gin_wait(i, dy)
         if i == 1:
@@ -349,7 +323,7 @@
 
         for dz in Z_FAR:
             hm_copy(dz).start()
-        w_wait(i, 1, home)
+        w_wait(i, 1)
         for dz in Z_ORDER:
             zz = lax.rem(z + dz, NZ)
             part = hm.at[i, pl.ds(pl.multiple_of(zz * HD, 128), HD)]
@@ -635,6 +609,7 @@
             step_done = layer_step(0)
             send_on(0)
             release()
+            release()
             sent = []
 
             @pl.when(s > 0)
@@ -662,7 +637,6 @@
 
         @pl.when(s < 3)
         def _():
-            release()
             sent = []
             gather(out, 1, sent, add_out)
             grad_ref[...] = out[own, :].astype(F32)
@@ -740,7 +714,7 @@
             pltpu.VMEM((FEATS, 1, SL), F32),
             pltpu.VMEM((2, NZ, HD, WIN), BF16),
             pltpu.VMEM((2, BLOCK, NZ * HD), BF16),
-            pltpu.VMEM((3, COLS, COLS), BF16),
+            pltpu.VMEM((2, COLS, COLS), BF16),
             pltpu.VMEM((2, BLOCK + 2 * PAD, COLS), BF16),
             pltpu.VMEM((2, NZ, HD, COLS), BF16),
             pltpu.VMEM((2, NZ, HD, COLS), BF16),
@@ -757,8 +731,10 @@
             dma((3, NZ)),
             dma((FEATS,)),
             dma((FEATS,)),
-            dma((2, 3, NZ)),
-            dma((2, 3, NZ)),
+            dma((2, NZ)),
+            dma((2, NZ)),
+            dma((2, 3)),
+            dma((2, 3)),
             dma((3, NY)),
             dma((2, NY)),
             dma((8,)),

time: 142 us -> 124 us (0.87)
  the two profiles are of different devices: /device:TPU:4 before, /device:TPU:1 now
where the time goes in v3:
time: 124 us; the launch traced here: 123 us
  Pallas kernels  121 us (98%)
  between operations  1.49 us (1%)
  local copies, waits for them, and re-layouts  1.35 us (1%)
    pallas_call x1, Pallas kernels, body(): pl.pallas_call(main_kernel, out_shape=(jax.ShapeDtypeStruct((features, CO...  118 us
    pallas_call x1, Pallas kernels, body(): pl.pallas_call(pick_kernel, out_shape=(jax.ShapeDtypeStruct((1, TGT, slot...  2.51 us

profile of v3, /device:TPU:1, one launch (start us, length us, event | category | flops | bytes accessed | tf_op | source)
XLA Modules:
  0.0 123.4 jit_solution(2153079344954257684)
XLA Ops:
  1.3 1.3 %reshape.10.tgain_hbm = f32[1,4608]{1,0:T(1,128)} reshape(f32[4608]{0:T(1024)} %param.19) | data formatting | bytes 36864 | tf_op jit(solution)/shard_map/reshape | solution.py:756
  2.6 118.1 %chain.1 = (f32[256,128]{1,0:T(8,128)}, f32[144,128]{1,0:T(8,128)}) custom-call(s32[8]{0:T(128)} %ids_hbm.2, s32[8]{0:T(128)} %pos_hbm.2, f32[1,4608]{1,0:T(1,128)} %reshape.10.tgain_hbm, f32[1,32]{1,0:T(1,128)} %bitcast.1, f32[1,4608]{1,0:T(1,128)} %pgain_hbm.1, f32[1,32]{1,0:T(1,128)} %pscale_hbm.1, f32[1,4608]{1,0:T(1,128)} %qgain_hbm.1, ...), custom_call_target="tpu_custom_call" | custom-call | tf_op jit(solution)/shard_map/chain/pallas_call | solution.py:682
  120.7 2.5 %pick.1 = (f32[1,4,16,128]{3,2,1,0:T(8,128)}, bf16[1,4,32,144]{3,2,1,0:T(8,128)(2,1)}) custom-call(s32[1,16]{1,0:T(1,128)} %pos_hbm.3, s32[1,1]{1,0:T(1,128)S(6)} %copy.19.count_hbm, s32[1,16,128]{2,1,0:T(8,128)} %ids_hbm.3, f32[1,16,128]{2,1,0:T(8,128)} %act_hbm.1, f32[256,128]{1,0:T(8,128)} %get-tuple-element.4.score_ref, f32[144,128]{1,0:T(8,128)} %get-tuple-element.5.grad_ref), custom_call_target="tpu_custom_call" | custom-call | tf_op jit(solution)/shard_map/pick/pallas_call | solution.py:760

commit v4 on v3

--- a/solution.py
+++ b/solution.py
@@ -21,6 +21,7 @@
 BLOCK = D // NZ
 WIN = 640
 PAD = WIN - BLOCK
+SPLIT = 96
 Z_ORDER = (1, 7, 2, 6, 3, 5, 4)
 Z_FAR = (4, 3, 5, 2, 6, 1, 7)
 Y_ORDER = (1, 3, 2)
@@ -32,10 +33,10 @@
     enc_hbm, out_hbm, val_hbm, dec_hbm,
     score_ref, grad_ref,
     ids_ref, pos_ref, tgain_ref, tscale_ref, pgain_ref, pscale_ref, qgain_ref, qscale_ref, pattern_ref,
-    enc, outp, val, dec, rows, rows0, top_own, e1, e2, e3, e2src, msg, recv, gslice, qslice,
+    enc, outp, val, dec, rows, rows0, top_own, epack, e1, e2, e3, e2src, msg, recv, gslice, qslice,
     ow, vw, mixw, gin, hsrc, hpart, hm, gsrc, gpart, res, up, out,
-    load_sem, small_sem, core_sem, e_send, e_recv, p_send, p_recv, w_send, w_recv, f_send, f_recv,
-    gin_send, gin_recv, attr_send, h_send, h_recv, m_send, m_recv, y_send, y_recv, g_send, g_recv, go_sem,
+    load_sem, small_sem, core_sem, e_send, e_recv, p_send, p_recv, w_send, w_recv, f_send, f_recv, o_send, o_recv,
+    gin_send, gin_recv, attr_send, h_send, h_recv, m_send, m_recv, y_send, y_recv, g_send, g_recv, l_send, l_recv, go_sem,
 ):
     s = lax.axis_index("section")
     f = lax.axis_index("feat")
@@ -57,7 +58,12 @@
             src_ref=src, dst_ref=dst, send_sem=ss, recv_sem=rs, device_id=dev, device_id_type=MESH
         )
 
-    load_enc = pltpu.make_async_copy(enc_hbm, enc, load_sem.at[0])
+    enc_part = enc.shape[0] // 4
+    load_enc = [
+        pltpu.make_async_copy(enc_hbm.at[pl.ds(k * enc_part, enc_part)], enc.at[pl.ds(k * enc_part, enc_part)],
+                              load_sem.at[4 + k])
+        for k in range(4)
+    ]
     load_out = pltpu.make_async_copy(out_hbm.at[0, 0], outp, load_sem.at[1])
     load_val = pltpu.make_async_copy(val_hbm.at[0, 0], val, load_sem.at[2])
     load_dec = pltpu.make_async_copy(dec_hbm.at[0], dec, load_sem.at[3])
@@ -68,54 +74,59 @@
 
     @pl.when(s == 3)
     def _():
-        load_enc.start()
+        for item in load_enc:
+            item.start()
+
+    barrier = pltpu.get_barrier_semaphore()
+
+    def hello(dev):
+        pl.semaphore_signal(barrier, inc=1, device_id=dev, device_id_type=MESH)
+
+    for dz in Z_FAR:
+        hello(zdev(dz))
+    for dy in Y_FAR:
+        hello(ydev(dy))
+
+    def column_peers(plane, core):
+        for dz in Z_FAR:
+            hello((plane, lax.rem(z + dz, NZ) * NY + y, core))
+
+    def row_peers(plane, core):
+        for dy in Y_FAR:
+            hello((plane, z * NY + lax.rem(y + dy, NY), core))
+
+    @pl.when((c == 0) & (s == 0))
+    def _():
+        column_peers(2, 1)
+        row_peers(2, 1)
+
+    @pl.when(c == 1)
+    def _():
+        @pl.when(s == 2)
+        def _():
+            column_peers(0, 0)
+            row_peers(0, 0)
+
+        for k in (2, 1, 3):
+            q = lax.rem(s + k, 4)
+            row_peers(q, 1)
+            hello((q, f, 1))
+
+    for q in range(4):
+        hello((q, f, 1 - c))
 
     for item in small:
         item.start()
-    load_out.start()
-    load_val.start()
-    load_dec.start()
-
-    barrier = pltpu.get_barrier_semaphore()
-
-    def hello(dev):
-        pl.semaphore_signal(barrier, inc=1, device_id=dev, device_id_type=MESH)
-
-    @pl.when(c == 0)
+
+    @pl.when((s < 3) & (c == 1))
     def _():
-        for dz in Z_ORDER:
-            hello(zdev(dz))
-        for dy in Y_ORDER:
-            hello(ydev(dy))
-
-    @pl.when(c == 1)
+        load_out.start()
+        load_val.start()
+
+    @pl.when((s < 3) & (c == 0))
     def _():
-        for dz in Z_ORDER:
-            hello(zdev(dz))
-        for dy in Y_ORDER:
-            hello(ydev(dy))
-
-        def other_planes(k, carry):
-            q = lax.rem(s + k, 4)
-            for dz in range(NZ):
-                hello((q, lax.rem(z + dz, NZ) * NY + y, 1))
-            for dy in Y_ORDER:
-                hello((q, z * NY + lax.rem(y + dy, NY), 1))
-            return carry
-
-        lax.fori_loop(1, 4, other_planes, 0)
-
-        @pl.when(s == 3)
-        def _():
-            def rest(dz, carry):
-                for dy in Y_ORDER:
-                    hello((s, lax.rem(z + dz, NZ) * NY + lax.rem(y + dy, NY), 1))
-                return carry
-
-            lax.fori_loop(1, NZ, rest, 0)
-
-    for q in range(4):
-        hello((q, f, 1 - c))
+        load_dec.start()
+
     for item in small:
         item.wait()
 
@@ -133,7 +144,15 @@
         return jnp.sum(jnp.where(eye, jnp.broadcast_to(row, (n, n)), 0.0), axis=1, keepdims=True)
 
     def pick_rows():
-        load_enc.wait()
+        for item in load_enc:
+            item.wait()
+
+        @pl.when(c == 1)
+        def _():
+            load_out.start()
+            load_val.start()
+
+        load_dec.start()
         base = (f * 2 + c) * enc.shape[0]
         wanted = jnp.full((8, 1), -1, jnp.int32)
         for t in range(8):
@@ -223,6 +242,18 @@
         dest = 2 if di == 1 else jnp.where(s == 1, 0, 3)
         return remote(ref, ref, f_send.at[di, kind], f_recv.at[home_slot, kind], (dest, f, 1))
 
+    def piece_copy(zz, di):
+        ref = ow.at[home_slot, zz]
+        dest = 2 if di == 1 else jnp.where(s == 1, 0, 3)
+        return remote(ref, ref, o_send.at[di, zz], o_recv.at[home_slot, zz], (dest, f, 1))
+
+    def piece_start(zz):
+        piece_copy(zz, 0).start()
+
+        @pl.when(s == 0)
+        def _():
+            piece_copy(zz, 1).start()
+
     def on_start(kind):
         on_copy(kind, 0).start()
 
@@ -231,13 +262,17 @@
             on_copy(kind, 1).start()
 
     def w_arrived(kind):
+        if kind == 0:
+            piece_start(z)
         for dz in Z_ORDER:
-            zz = lax.rem(z + dz, NZ)
+            zz = lax.rem(z + NZ - dz, NZ)
             if kind == 0:
                 part = ow.at[home_slot, zz]
             else:
                 part = vw.at[home_slot, :, pl.ds(pl.multiple_of(zz * HD, 128), HD)]
             remote(part, part, w_send.at[kind, 0], w_recv.at[kind, zz], ydev(1)).wait_recv()
+            if kind == 0:
+                piece_start(zz)
 
     def weights_start():
         load_out.wait()
@@ -256,34 +291,89 @@
         for k in range(FEATS):
             part = slice(k * SL, (k + 1) * SL)
             val[part, :] = (val[part, :].astype(F32) * column(qgain_ref[:, part])).astype(BF16)
+
+        @pl.when(s == 2)
+        def _():
+            raw_copy().start()
+
         for dz in Z_FAR:
             w_copy(dz, 1).start()
         vw[home_slot, :, pl.ds(pl.multiple_of(z * HD, 128), HD)] = val[pl.ds(pl.multiple_of(z * BLOCK, 16), BLOCK), :]
         w_arrived(0)
-        on_start(0)
-        w_arrived(1)
-        on_start(1)
+
+        @pl.when(s < 2)
+        def _():
+            w_arrived(1)
+            on_start(1)
+
+    def raw_copy():
+        return remote(val, up, f_send.at[0, 1], f_recv.at[0, 1], (3, f, 1))
+
+    def raw_part(dz):
+        zz = lax.rem(z + dz, NZ)
+        src = up.at[pl.ds(pl.multiple_of(zz * BLOCK, 16), BLOCK)]
+        dst = vw.at[0, :, pl.ds(pl.multiple_of(z * HD, 128), HD)]
+        return remote(src, dst, w_send.at[1, dz], w_recv.at[1, z], zdev(dz))
+
+    def raw_start():
+        raw_copy().wait_recv()
+        for dz in Z_FAR:
+            raw_part(dz).start()
+        vw[0, :, pl.ds(pl.multiple_of(z * HD, 128), HD)] = up[pl.ds(pl.multiple_of(z * BLOCK, 16), BLOCK), :]
+
+    def raw_done():
+        for dz in Z_FAR:
+            raw_part(dz).wait_send()
 
     def weights_done():
         for kind in range(2):
             for dz in Z_FAR:
                 w_copy(dz, kind).wait_send()
-        for kind in range(3):
-            on_copy(kind, 0).wait_send()
+        @pl.when(s == 2)
+        def _():
+            raw_copy().wait_send()
+
+        @pl.when(s < 2)
+        def _():
+            on_copy(1, 0).wait_send()
+
+        on_copy(2, 0).wait_send()
+
+        @pl.when(s == 0)
+        def _():
+            on_copy(1, 1).wait_send()
+            on_copy(2, 1).wait_send()
+
+        for zz in range(NZ):
+            piece_copy(zz, 0).wait_send()
 
             @pl.when(s == 0)
             def _():
-                on_copy(kind, 1).wait_send()
+                piece_copy(zz, 1).wait_send()
 
     def w_wait(i, kind):
         def one():
+            if kind == 0:
+                for zz in range(NZ):
+                    ref = ow.at[i, zz]
+                    remote(ref, ref, o_send.at[0, 0], o_recv.at[i, zz], ydev(1)).wait_recv()
+                return
             ref = (ow, vw, mixw)[kind].at[i]
             remote(ref, ref, f_send.at[0, kind], f_recv.at[i, kind], ydev(1)).wait_recv()
 
         if i == 1:
             one()
+        elif kind != 1:
+            pl.when((s == 0) | (s == 3))(one)
         else:
-            pl.when((s == 0) | (s == 3))(one)
+            pl.when(s == 0)(one)
+
+            @pl.when(s >= 2)
+            def _():
+                for dz in Z_ORDER:
+                    zz = lax.rem(z + dz, NZ)
+                    part = vw.at[0, :, pl.ds(pl.multiple_of(zz * HD, 128), HD)]
+                    remote(part, part, w_send.at[1, 0], w_recv.at[1, zz], ydev(1)).wait_recv()
 
     def layer_step(i):
         gin[i, 0:PAD] = jnp.zeros((PAD, COLS), BF16)
@@ -360,26 +450,33 @@
     def top_layer():
         me = y
 
-        def quarter(j):
-            return rows.at[:, pl.ds(pl.multiple_of(j * QUARTER, 128), QUARTER)]
+        def packed(value):
+            rest = jnp.concatenate([value[:, WIN:], jnp.zeros((8, 2 * WIN - QUARTER), F32)], axis=1)
+            return jnp.concatenate([value[:, :WIN], rest], axis=0).astype(BF16)
+
+        def unpacked(value):
+            value = value.astype(F32)
+            return jnp.concatenate([value[:8], value[8:, :QUARTER - WIN]], axis=1)
 
         def e_copy(stage, src, dst, k, slot, dev):
             return remote(src, dst.at[slot], e_send.at[stage, k], e_recv.at[stage, slot], dev)
 
         remote(rows0, rows0, core_sem.at[0], core_sem.at[1], (s, f, 0)).wait_recv()
         rows[...] = rows[...] + rows0[...]
+        for k in range(NY):
+            epack[k] = packed(rows[:, k * QUARTER:(k + 1) * QUARTER])
 
         def e1_copy(dy):
-            return e_copy(0, quarter(lax.rem(y + dy, NY)), e1, dy, me, ydev(dy))
+            return e_copy(0, epack.at[lax.rem(y + dy, NY)], e1, dy, me, ydev(dy))
 
         for dy in Y_FAR:
             e1_copy(dy).start()
-        total = quarter(me)[...]
+        total = epack[me].astype(F32)
         for dy in Y_ORDER:
             j = lax.rem(y + dy, NY)
             e_copy(0, e2src, e1, 0, j, ydev(1)).wait_recv()
-            total = total + e1[j]
-        e2src[...] = total
+            total = total + e1[j].astype(F32)
+        e2src[...] = total.astype(BF16)
 
         def e2_copy(dz):
             return e_copy(1, e2src, e2, dz, z, zdev(dz))
@@ -389,8 +486,8 @@
         for dz in Z_ORDER:
             j = lax.rem(z + dz, NZ)
             e_copy(1, e2src, e2, 0, j, ydev(1)).wait_recv()
-            total = total + e2[j]
-        e3[me] = total
+            total = total + e2[j].astype(F32)
+        e3[me] = total.astype(BF16)
 
         def e3_copy(dy):
             return e_copy(2, e3.at[me], e3, dy, me, ydev(dy))
@@ -399,9 +496,7 @@
             e3_copy(dy).start()
         for dy in Y_ORDER:
             e_copy(2, e2src, e3, 0, lax.rem(y + dy, NY), ydev(1)).wait_recv()
-        for dy in Y_FAR:
-            e1_copy(dy).wait_send()
-        raw = jnp.concatenate([e3[k] for k in range(NY)], axis=1)
+        raw = jnp.concatenate([unpacked(e3[k]) for k in range(NY)], axis=1)
 
         tops, scaled, at_rows, lanes = [], [], [], []
         pattern4 = jnp.concatenate([pattern] * TGT, axis=1)
@@ -430,26 +525,33 @@
         load_val.wait()
         gap = jnp.zeros((SEQ - (SL - HD), HD), BF16)
 
+        order = [(dz, dy) for dz in Z_FAR + (0,) for dy in Y_FAR + (0,)]
+
         def m_copy(k):
-            return remote(msg.at[lax.rem(f + k, FEATS)], recv.at[f], p_send.at[k], p_recv.at[f], fdev(k))
-
-        for k in range(FEATS):
-            tail = val[k * SL + HD:(k + 1) * SL, :]
-            weights = jnp.concatenate([val[k * SL:k * SL + HD, :]] + [tail, gap] * TGT, axis=0)
+            dz, dy = order[k]
+            to = lax.rem(z + dz, NZ) * NY + lax.rem(y + dy, NY)
+            return remote(msg.at[to], recv.at[f], p_send.at[k], p_recv.at[f], (s, to, 1))
+
+        for k, (dz, dy) in enumerate(order):
+            to = lax.rem(z + dz, NZ) * NY + lax.rem(y + dy, NY)
+            main = val[pl.ds(pl.multiple_of(to * SL, 16), HD), :]
+            tail = val[pl.ds(pl.multiple_of(to * SL + HD, 16), SL - HD), :]
+            weights = jnp.concatenate([main] + [tail, gap] * TGT, axis=0)
             got = lax.dot_general(head_in, weights, NT, preferred_element_type=F32)
+            parts = []
             for group in range(2):
                 part = got[8 * group:8 * group + 8]
                 spread = jnp.where(lane_t == (row_t + 1) % TGT, part[:, HD:], 0.0)
                 low = pltpu.roll(spread + at_rows[group], TGT, 0)
-                msg[k, 8 * group:8 * group + 8] = jnp.where(row_t < TGT, part[:, :HD], low)
-
-        def m_start(k, carry):
-            m_copy(k).start()
-            return carry
-
-        lax.fori_loop(1, FEATS, m_start, 0)
-        recv[f] = msg[f]
+                parts.append(jnp.where(row_t < TGT, part[:, :HD], low))
+            value = jnp.concatenate(parts, axis=0).astype(BF16)
+            if k == len(order) - 1:
+                recv[f] = value
+            else:
+                msg[to] = value
+                m_copy(k).start()
         top_copy.start()
+        raw_start()
         for k in range(FEATS):
             qslice[k] = qgain_ref[:, k * SL:(k + 1) * SL]
         gain = column(qslice[f])
@@ -467,7 +569,7 @@
         lax.fori_loop(1, FEATS, m_wait_one, 0)
         tail_t = lax.broadcasted_iota(jnp.int32, (SL - HD, COLS), 1) // SEQ
         for group in range(2):
-            got = recv[:, 8 * group:8 * group + 8, :].reshape(FEATS * 8, COLS)
+            got = recv[...].astype(F32)[:, 8 * group:8 * group + 8, :].reshape(FEATS * 8, COLS)
             got_row = lax.broadcasted_iota(jnp.int32, got.shape, 0) % 8
             got_t = lax.broadcasted_iota(jnp.int32, got.shape, 1) // SEQ
             low = jnp.where((got_row >= TGT) & (got_t == got_row - TGT), got, 0.0)
@@ -496,6 +598,7 @@
 
         def done():
             for dy in Y_FAR:
+                e1_copy(dy).wait_send()
                 e3_copy(dy).wait_send()
                 gin_copy(res.at[3], 3, dy, 0, 1).wait_send()
             for dy in range(NY):
@@ -503,14 +606,12 @@
             for dz in Z_FAR:
                 e2_copy(dz).wait_send()
             top_copy.wait_send()
+            raw_done()
             for item in notes:
                 item.wait_send()
 
-            def m_done(k, carry):
+            for k in range(FEATS - 1):
                 m_copy(k).wait_send()
-                return carry
-
-            lax.fori_loop(1, FEATS, m_done, 0)
 
         return done
 
@@ -522,6 +623,59 @@
     layer_now = jnp.where(s >= 2, 2, 1)
     group_now = jnp.where((s == 1) | (s == 2), 0, 1)
 
+    def last_z(dz):
+        dev = (0, lax.rem(z + dz, NZ) * NY + y, s - 2)
+        dst = out.at[pl.ds(pl.multiple_of(f * SL, 16), SPLIT)]
+        return remote(res.at[1, pl.ds(0, SPLIT)], dst, l_send.at[dz], g_recv.at[1, f], dev)
+
+    def last_y(dy):
+        dev = (0, z * NY + lax.rem(y + dy, NY), s - 2)
+        dst = out.at[pl.ds(pl.multiple_of(f * SL + SPLIT, 16), SL - SPLIT)]
+        return remote(res.at[1, pl.ds(SPLIT, SL - SPLIT)], dst, l_send.at[NZ + dy], l_recv.at[f], dev)
+
+    def last_gather(sent):
+        def copy(part, b, dev, i):
+            if part == 0:
+                ref = out.at[pl.ds(pl.multiple_of(b * SL, 16), SPLIT)]
+                return remote(ref, ref, g_send.at[1, i], g_recv.at[1, b], dev)
+            ref = out.at[pl.ds(pl.multiple_of(b * SL + SPLIT, 16), SL - SPLIT)]
+            return remote(ref, ref, l_send.at[i], l_recv.at[b], dev)
+
+        def start(item):
+            item.start()
+            sent.append(item)
+
+        def relay_y(i, dz):
+            b = lax.rem(z + NZ - dz, NZ) * NY + y
+            copy(0, b, ydev(1), 0).wait_recv()
+            for j, dy in enumerate(Y_FAR):
+                start(copy(0, b, ydev(dy), 3 * i + j))
+
+        def relay_z(i, dy):
+            b = z * NY + lax.rem(y + dy, NY)
+            copy(1, b, ydev(1), 0).wait_recv()
+            for j, dz in enumerate(Z_FAR):
+                start(copy(1, b, zdev(dz), 7 * i + j))
+
+        zs = (0,) + Z_ORDER
+        ys = (0,) + Y_ORDER
+        for i in range(NZ):
+            if i % 2 == 0:
+                relay_z(i // 2, ys[i // 2])
+            relay_y(i, zs[i])
+        span = 2 * NY * SL
+        for dq in (0, 1, 3, 2):
+            q = lax.rem(z // 2 + dq, NZ // 2)
+            for half in range(2):
+                zz = 2 * q + half if dq else jnp.where(half == 0, z, z + 1 - 2 * (z % 2))
+                for dy in Y_ORDER:
+                    copy(0, zz * NY + lax.rem(y + dy, NY), ydev(1), 0).wait_recv()
+                if dq or half:
+                    for dy in ys:
+                        copy(1, zz * NY + lax.rem(y + dy, NY), ydev(1), 0).wait_recv()
+            part = pl.ds(pl.multiple_of(q * span, 128), span)
+            add_out(part, out[part, :])
+
     def send_copies():
         items = [gin_copy(res.at[0], to_plane, dy, gin_slot, 2) for dy in (2, 1, 3, 0)]
         return items + [attribution_copy(res.at[0], out, 1, layer_now, group_now, 3)]
@@ -548,6 +702,21 @@
         @pl.when(s > 0)
         def _():
             up_copy().wait_send()
+
+    def out_gather():
+        @pl.when(s == 0)
+        def _():
+            sent = []
+            last_gather(sent)
+            finish(sent)
+
+        @pl.when(s > 0)
+        def _():
+            sent = []
+            gather(out, 1, sent, add_out)
+            finish(sent)
+
+        grad_ref[...] = out[own, :].astype(F32)
 
     @pl.when(c == 0)
     def _():
@@ -565,7 +734,14 @@
 
         @pl.when(s < 3)
         def _():
-            pl.semaphore_wait(barrier, 14)
+            @pl.when(s == 0)
+            def _():
+                pl.semaphore_wait(barrier, 24)
+
+            @pl.when(s > 0)
+            def _():
+                pl.semaphore_wait(barrier, 14)
+
             score_ref[...] = jnp.zeros_like(score_ref)
             load_dec.wait()
             sent = []
@@ -574,19 +750,14 @@
             pl.semaphore_wait(go_sem, 1)
             finish(sent)
 
-        sent = []
-        gather(out, 1, sent, add_out)
-        grad_ref[...] = out[own, :].astype(F32)
-        finish(sent)
-        load_out.wait()
-        load_val.wait()
+        out_gather()
 
     @pl.when(c == 1)
     def _():
         @pl.when(s == 3)
         def _():
             pick_rows()
-            pl.semaphore_wait(barrier, 68)
+            pl.semaphore_wait(barrier, 26)
             top_done = top_layer()
             load_dec.wait()
             step_done = layer_step(0)
@@ -602,8 +773,16 @@
 
         @pl.when(s < 3)
         def _():
-            pl.semaphore_wait(barrier, 47)
+            @pl.when(s == 2)
+            def _():
+                pl.semaphore_wait(barrier, 36)
+
+            @pl.when(s < 2)
+            def _():
+                pl.semaphore_wait(barrier, 26)
+
             weights_start()
+            load_dec.start()
             score_ref[...] = jnp.zeros_like(score_ref)
             load_dec.wait()
             step_done = layer_step(0)
@@ -630,17 +809,15 @@
         @pl.when(s >= 2)
         def _():
             step_done = layer_step(1)
-            last = attribution_copy(res.at[1], out, 1, 0, s - 2, 6)
-            last.start()
+            last = [last_z(dz) for dz in Z_FAR + (0,)] + [last_y(dy) for dy in Y_FAR + (0,)]
+            for item in last[:7:2] + last[8:11] + last[1:8:2] + last[11:]:
+                item.start()
             step_done()
-            last.wait_send()
+            finish(last)
 
         @pl.when(s < 3)
         def _():
-            sent = []
-            gather(out, 1, sent, add_out)
-            grad_ref[...] = out[own, :].astype(F32)
-            finish(sent)
+            out_gather()
 
         send_done()
 
@@ -704,12 +881,13 @@
             pltpu.VMEM((8, D), F32),
             pltpu.VMEM((8, D), F32),
             pltpu.VMEM((8, D), F32),
-            pltpu.VMEM((NY, 8, QUARTER), F32),
-            pltpu.VMEM((NZ, 8, QUARTER), F32),
-            pltpu.VMEM((NY, 8, QUARTER), F32),
-            pltpu.VMEM((8, QUARTER), F32),
-            pltpu.VMEM((FEATS, 16, COLS), F32),
-            pltpu.VMEM((FEATS, 16, COLS), F32),
+            pltpu.VMEM((NY, 16, WIN), BF16),
+            pltpu.VMEM((NY, 16, WIN), BF16),
+            pltpu.VMEM((NZ, 16, WIN), BF16),
+            pltpu.VMEM((NY, 16, WIN), BF16),
+            pltpu.VMEM((16, WIN), BF16),
+            pltpu.VMEM((FEATS, 16, COLS), BF16),
+            pltpu.VMEM((FEATS, 16, COLS), BF16),
             pltpu.VMEM((FEATS, 8, SL), F32),
             pltpu.VMEM((FEATS, 1, SL), F32),
             pltpu.VMEM((2, NZ, HD, WIN), BF16),
@@ -724,7 +902,7 @@
             pltpu.VMEM((4, SL, COLS), BF16),
             pltpu.VMEM((D, COLS), BF16),
             pltpu.VMEM((D, COLS), BF16),
-            dma((4,)),
+            dma((8,)),
             dma((9,)),
             dma((2,)),
             dma((3, NZ)),
@@ -735,6 +913,8 @@
             dma((2, NZ)),
             dma((2, 3)),
             dma((2, 3)),
+            dma((2, NZ)),
+            dma((2, NZ)),
             dma((3, NY)),
             dma((2, NY)),
             dma((8,)),
@@ -746,6 +926,8 @@
             dma((2, NY)),
             dma((2, FEATS)),
             dma((2, FEATS)),
+            dma((FEATS,)),
+            dma((FEATS,)),
             pltpu.SemaphoreType.REGULAR,
         ],
         compiler_params=pltpu.CompilerParams(

time: 124 us -> 117 us (0.944)
  Pallas kernels: 121 us -> 114 us
    pallas_call x1, Pallas kernels: 118 us -> 111 us  [body(): pl.pallas_call(main_kernel, out_shape=(jax.ShapeDtypeStruct((features, CO...]
where the time goes in v4:
time: 117 us; the launch traced here: 116 us
  Pallas kernels  114 us (97%)
  between operations  1.49 us (1%)
  local copies, waits for them, and re-layouts  1.35 us (1%)
    pallas_call x1, Pallas kernels, body(): pl.pallas_call(main_kernel, out_shape=(jax.ShapeDtypeStruct((features, CO...  111 us
    pallas_call x1, Pallas kernels, body(): pl.pallas_call(pick_kernel, out_shape=(jax.ShapeDtypeStruct((1, TGT, slot...  2.51 us

profile of v4, /device:TPU:1, one launch (start us, length us, event | category | flops | bytes accessed | tf_op | source)
XLA Modules:
  0.0 116.5 jit_solution(14583421044865830456)
XLA Ops:
  1.3 1.3 %reshape.10.tgain_hbm = f32[1,4608]{1,0:T(1,128)} reshape(f32[4608]{0:T(1024)} %param.19) | data formatting | bytes 36864 | tf_op jit(solution)/shard_map/reshape | solution.py:938
  2.6 111.1 %chain.1 = (f32[256,128]{1,0:T(8,128)}, f32[144,128]{1,0:T(8,128)}) custom-call(s32[8]{0:T(128)} %ids_hbm.2, s32[8]{0:T(128)} %pos_hbm.2, f32[1,4608]{1,0:T(1,128)} %reshape.10.tgain_hbm, f32[1,32]{1,0:T(1,128)} %bitcast.1, f32[1,4608]{1,0:T(1,128)} %pgain_hbm.1, f32[1,32]{1,0:T(1,128)} %pscale_hbm.1, f32[1,4608]{1,0:T(1,128)} %qgain_hbm.1, ...), custom_call_target="tpu_custom_call" | custom-call | tf_op jit(solution)/shard_map/chain/pallas_call | solution.py:859
  113.8 2.5 %pick.1 = (f32[1,4,16,128]{3,2,1,0:T(8,128)}, bf16[1,4,32,144]{3,2,1,0:T(8,128)(2,1)}) custom-call(s32[1,16]{1,0:T(1,128)} %pos_hbm.3, s32[1,1]{1,0:T(1,128)S(6)} %copy.19.count_hbm, s32[1,16,128]{2,1,0:T(8,128)} %ids_hbm.3, f32[1,16,128]{2,1,0:T(8,128)} %act_hbm.1, f32[256,128]{1,0:T(8,128)} %get-tuple-element.4.score_ref, f32[144,128]{1,0:T(8,128)} %get-tuple-element.5.grad_ref), custom_call_target="tpu_custom_call" | custom-call | tf_op jit(solution)/shard_map/pick/pallas_call | solution.py:942

commit v5 on v4

--- a/solution.py
+++ b/solution.py
@@ -22,6 +22,7 @@
 WIN = 640
 PAD = WIN - BLOCK
 SPLIT = 96
+GROUP = 32
 Z_ORDER = (1, 7, 2, 6, 3, 5, 4)
 Z_FAR = (4, 3, 5, 2, 6, 1, 7)
 Y_ORDER = (1, 3, 2)
@@ -510,7 +511,7 @@
                               axis=1, keepdims=True)
             p_scale = jnp.sum(jnp.where(at_pos, jnp.broadcast_to(pscale_ref[...], (8, SEQ)), 0.0),
                               axis=1, keepdims=True)
-            top = (part * tgain_ref[...] * t_scale).astype(BF16).astype(F32)
+            top = (part * tgain_ref[...].reshape(1, D) * t_scale).astype(BF16).astype(F32)
             tops.append(top)
             scaled.append(top * pgain_ref[...] * p_scale)
             at_row = jnp.dot(at_pos.astype(BF16), pattern4.astype(BF16), preferred_element_type=F32)
@@ -533,6 +534,9 @@
             return remote(msg.at[to], recv.at[f], p_send.at[k], p_recv.at[f], (s, to, 1))
 
         for k, (dz, dy) in enumerate(order):
+            if k % GROUP == 0:
+                for e in range(max(k - GROUP, 0), k):
+                    m_copy(e).start()
             to = lax.rem(z + dz, NZ) * NY + lax.rem(y + dy, NY)
             main = val[pl.ds(pl.multiple_of(to * SL, 16), HD), :]
             tail = val[pl.ds(pl.multiple_of(to * SL + HD, 16), SL - HD), :]
@@ -549,7 +553,8 @@
                 recv[f] = value
             else:
                 msg[to] = value
-                m_copy(k).start()
+        for e in range((FEATS - 1) // GROUP * GROUP, FEATS - 1):
+            m_copy(e).start()
         top_copy.start()
         raw_start()
         for k in range(FEATS):
@@ -822,15 +827,18 @@
         send_done()
 
 
-def pick_kernel(pos_hbm, count_hbm, ids_hbm, act_hbm, score_ref, grad_ref, out_ref, grad_out_ref,
-                pos_ref, count_ref, ids_ref, act_ref, turned, picked, sem):
-    pairs = ((pos_hbm, pos_ref), (count_hbm, count_ref), (ids_hbm, ids_ref), (act_hbm, act_ref))
+def pick_kernel(pos_hbm, count_hbm, ids_hbm, act_hbm, score_hbm, grad_hbm, out_ref, grad_out_ref,
+                pos_ref, count_ref, ids_ref, act_ref, score_ref, grad_ref, turned, picked, sem):
+    pairs = ((score_hbm, score_ref), (grad_hbm, grad_ref), (pos_hbm, pos_ref), (count_hbm, count_ref),
+             (ids_hbm, ids_ref), (act_hbm, act_ref))
     copies = [pltpu.make_async_copy(src, dst, sem.at[i]) for i, (src, dst) in enumerate(pairs)]
     for item in copies:
         item.start()
+    copies[0].wait()
     turned[...] = score_ref[...].T
+    copies[1].wait()
     grad_out_ref[0] = grad_ref[...].T.astype(BF16).reshape(TGT, SEQ, SL)
-    for item in copies:
+    for item in copies[2:]:
         item.wait()
     slots, width = ids_ref.shape[1], ids_ref.shape[2]
     for b in range(slots):
@@ -867,7 +875,7 @@
         scratch_shapes=[
             pltpu.SMEM((2 * TGT,), jnp.int32),
             pltpu.SMEM((2 * TGT,), jnp.int32),
-            pltpu.VMEM((1, D), F32),
+            pltpu.VMEM((D,), F32),
             pltpu.VMEM((1, SEQ), F32),
             pltpu.VMEM((1, D), F32),
             pltpu.VMEM((1, SEQ), F32),
@@ -935,7 +943,7 @@
         ),
         name="chain",
     )(
-        target_ids, target_pos, target_gain.reshape(1, D), target_scale.reshape(1, SEQ), post_gain, post_scale,
+        target_ids, target_pos, target_gain, target_scale.reshape(1, SEQ), post_gain, post_scale,
         pre_gain, pre_scale, pattern, encoder, out_proj, value_proj, decoder,
     )
     slots, width = block_ids.shape[1], block_ids.shape[2]
@@ -945,16 +953,18 @@
             jax.ShapeDtypeStruct((1, TGT, slots, width), F32),
             jax.ShapeDtypeStruct((1, TGT, SEQ, SL), BF16),
         ),
-        in_specs=[hbm] * 4 + [vmem] * 2,
+        in_specs=[hbm] * 6,
         out_specs=(vmem, vmem),
         scratch_shapes=[
             pltpu.SMEM((1, slots), jnp.int32),
             pltpu.SMEM((1, 1), jnp.int32),
             pltpu.VMEM((1, slots, width), jnp.int32),
             pltpu.VMEM((1, slots, width), F32),
+            pltpu.VMEM((features, COLS), F32),
+            pltpu.VMEM((SL, COLS), F32),
             pltpu.VMEM((COLS, features), F32),
             pltpu.VMEM((TGT, slots, features), F32),
-            dma((4,)),
+            dma((6,)),
         ],
         name="pick",
     )(block_pos, block_count, block_ids, block_act, scores, grads)

time: 117 us -> 115 us (0.983)
  local copies, waits for them, and re-layouts: 1.35 us -> 0 us
    reshape x1 -> x0, local copies, waits for them, and re-layouts: 1.35 us -> none  [body(): target_gain.reshape(1, D)]
where the time goes in v5:
time: 115 us
  Pallas kernels  113 us (98%)
  between operations  1.49 us (1%)
    pallas_call x1, Pallas kernels, body(): pl.pallas_call(main_kernel, out_shape=(jax.ShapeDtypeStruct((features, CO...  111 us

profile of v5, /device:TPU:1, one launch (start us, length us, event | category | flops | bytes accessed | tf_op | source)
XLA Modules:
  0.0 115.0 jit_solution(3046985612986840403)
XLA Ops:
  1.3 111.5 %chain.1 = (f32[256,128]{1,0:T(8,128)}, f32[144,128]{1,0:T(8,128)}) custom-call(s32[8]{0:T(128)} %ids_hbm.2, s32[8]{0:T(128)} %pos_hbm.2, f32[4608]{0:T(1024)} %tgain_hbm.1, f32[1,32]{1,0:T(1,128)} %bitcast.1, f32[1,4608]{1,0:T(1,128)} %pgain_hbm.1, f32[1,32]{1,0:T(1,128)} %pscale_hbm.1, f32[1,4608]{1,0:T(1,128)} %qgain_hbm.1, f32[1,32]{1,0:T(1,128)} %qscale_hbm.1, ...), custom_call_target="tpu_custom_call" | custom-call | tf_op jit(solution)/shard_map/chain/pallas_call | solution.py:867
  112.8 2.0 %pick.1 = (f32[1,4,16,128]{3,2,1,0:T(8,128)}, bf16[1,4,32,144]{3,2,1,0:T(8,128)(2,1)}) custom-call(s32[1,16]{1,0:T(1,128)} %pos_hbm.3, s32[1,1]{1,0:T(1,128)S(6)} %copy.19.count_hbm, s32[1,16,128]{2,1,0:T(8,128)} %ids_hbm.3, f32[1,16,128]{2,1,0:T(8,128)} %act_hbm.1, f32[256,128]{1,0:T(8,128)} %get-tuple-element.4.score_hbm, f32[144,128]{1,0:T(8,128)} %get-tuple-element.5.grad_hbm), custom_call_target="tpu_custom_call" | custom-call | tf_op jit(solution)/shard_map/pick/pallas_call | solution.py:950
